TPU v7x, 32 devices: a whole 2x2x4 slice. The times are simulated.
32 devices in a mesh: dp: 4 (over z), seq: 8 (over y, x, core).
Axes of the slice: x: 2, y: 2, z: 4, core: 2. Of those that a mesh axis runs over, the one named last changes fastest.
Arguments:
- tokens: bfloat16 [4, 12288, 1024], P('dp', 'seq'), may hold values from -6 to 6
- image_tokens: bfloat16 [4, 1024, 768], P('dp', 'seq'), may hold values from -51 to 51
- norm_gain: float32 [1024], replicated, may hold values from 0.1 to 1.9
- w_query: bfloat16 [1024, 1024], replicated, may hold values from -0.1875 to 0.1875
- w_key: bfloat16 [768, 1024], replicated, may hold values from -0.21875 to 0.21875
- w_value: bfloat16 [768, 1024], replicated, may hold values from -0.21875 to 0.21875
- w_out: bfloat16 [1024, 1024], replicated, may hold values from -0.1875 to 0.1875
- w_plane: bfloat16 [1024, 80], replicated, may hold values from -0.1875 to 0.1875
- dec_w1: bfloat16 [64, 80], replicated, may hold values from -0.625 to 0.625
- dec_b1: float32 [64], replicated, may hold values from -3 to 3
- dec_w2: bfloat16 [64, 64], replicated, may hold values from -0.75 to 0.75
- dec_b2: float32 [64], replicated, may hold values from -3 to 3
- dec_w3: bfloat16 [4, 64], replicated, may hold values from -0.75 to 0.75
- dec_b3: float32 [4], replicated, may hold values from -3 to 3
- corner_idx: int32 [4, 12, 32768], P('dp', None, 'seq'), may hold values from 0 to 12287, as said below
- corner_wts: bfloat16 [4, 12, 32768], P('dp', None, 'seq'), may hold values from 0 to 1, as said below
- target_color: float32 [4, 3, 256], P('dp', None, 'seq'), may hold values from 0 to 1
Outputs:
- colors: float32 [4, 3, 256], P('dp', None, 'seq')
- token_grad: bfloat16 [4, 12288, 1024], P('dp', 'seq')
- plane_weight_grad: float32 [1024, 80], replicated
Inputs may be any that keep to these rules, and one draw needn't show every extreme that they name: `corner_idx`: each entry names a triplane token of the scene; for each sample and plane the four entries are the corners of one grid cell of that plane, and consecutive samples of a ray walk through neighbouring cells. `corner_wts`: for each sample and plane the four weights are the bilinear weights of one point in that cell.
All inputs are finite; a program needn't handle non-finite values.
Results may differ from a plain program's by a relative error of at most 0.017.
Values may be sent and summed in bfloat16 or wider, within the bound.
No kernel may reach another device: no remote copies, remote signals or barrier semaphores. Data moves between devices by JAX's collectives and lax.ppermute only.
A program may use at most 128 MiB of HBM per device.

v0:
```python
import functools
import math

import jax
import jax.numpy as jnp
from jax import lax
from jax.experimental import pallas as pl
from jax.experimental.pallas import tpu as pltpu
from jax.sharding import PartitionSpec as P

HEADS = 16
STEPS = 128
PLANES = 3
LANES = 128
TILE_RAYS = 32
TOGETHER = 4

NORM_EPS = 1e-05
DEPTH_STEP = 0.02
MIB = 1024 * 1024
VMEM_BYTES = 56 * MIB

F32 = jnp.float32
BF16 = jnp.bfloat16


def contract(left, right, left_dim, right_dim, out_type=F32, precision=None):
    return lax.dot_general(
        left,
        right,
        (((left_dim,), (right_dim,)), ((), ())),
        preferred_element_type=out_type,
        precision=precision,
    )


def plain_norm(inputs):
    row_mean = jnp.mean(inputs, axis=-1, keepdims=True)
    centred = inputs - row_mean
    row_var = jnp.mean(centred * centred, axis=-1, keepdims=True)
    return centred * lax.rsqrt(row_var + NORM_EPS)


def params(vmem_bytes=VMEM_BYTES):
    return pltpu.CompilerParams(vmem_limit_bytes=vmem_bytes)


def swap(array, axis, distance):
    pairs = [(i, i ^ distance) for i in range(lax.axis_size(axis))]
    return lax.ppermute(array, axis, pairs)


def from_chips(piece):
    return [swap(piece, "seq", k) for k in range(2, lax.axis_size("seq"), 2)]


def with_other_core(pieces):
    return [each for piece in pieces for each in (piece, swap(piece, "seq", 1))]


def gather_scene(piece):
    return with_other_core([piece]) + with_other_core(from_chips(piece))


def whole(shape):
    return pl.BlockSpec(shape, lambda step: (0,) * len(shape), pipeline_mode=pl.Buffered(1))


def kept(shape):
    return pl.BlockSpec(shape, lambda step: (0,) * len(shape))


def estimate(flops, bytes_accessed):
    return pl.CostEstimate(flops=flops, bytes_accessed=bytes_accessed, transcendentals=0)


def query_kernel(query_scale, tokens_ref, w_query_ref, queries_ref):
    normed = plain_norm(tokens_ref[...].astype(F32)).astype(BF16)
    queries = jnp.dot(normed, w_query_ref[...], preferred_element_type=F32)
    queries_ref[...] = (queries * query_scale).astype(BF16)


def query_call(tokens, w_query, query_scale):
    rows, width = tokens.shape
    tile = math.gcd(rows, 512)
    return pl.pallas_call(
        functools.partial(query_kernel, query_scale),
        grid=(rows // tile,),
        in_specs=[pl.BlockSpec((tile, width), lambda step: (step, 0)), whole(w_query.shape)],
        out_specs=pl.BlockSpec((tile, width), lambda step: (step, 0)),
        out_shape=jax.ShapeDtypeStruct((rows, width), BF16),
        cost_estimate=estimate(2 * rows * width * width, 4 * rows * width),
        compiler_params=params(32 * MIB),
        name="queries",
    )(tokens, w_query)


def attend_kernel(head_dim, shares, *refs):
    image_refs, refs = refs[:shares], refs[shares:]
    w_key_ref, w_value_ref, tokens_ref, queries_ref, w_out_ref, gain_ref, w_plane_ref = refs[:7]
    plane_in_ref, planes_ref, keys_ref, values_ref, attended_ref = refs[7:]
    rows, width = tokens_ref.shape
    groups = width // LANES

    @pl.when(pl.program_id(0) == 0)
    def project_images():
        images = jnp.concatenate([ref[...] for ref in image_refs], axis=0)
        keys = jnp.dot(images, w_key_ref[...], preferred_element_type=F32).astype(BF16)
        keys_ref[...] = keys.T
        values = jnp.dot(images, w_value_ref[...], preferred_element_type=F32).astype(BF16)
        ones = jnp.ones((values.shape[0], LANES), BF16)
        for group in range(groups):
            values_ref[group, :, :LANES] = values[:, group * LANES : (group + 1) * LANES]
            values_ref[group, :, LANES:] = ones

    lane_ids = lax.broadcasted_iota(jnp.int32, (rows, LANES), 1)
    together = math.gcd(groups, TOGETHER)
    heads = [(group, low) for group in range(together) for low in range(0, LANES, head_dim)]

    def own_lanes(low):
        return (lane_ids >= low) & (lane_ids < low + head_dim)

    def group_step(step, _):
        def columns(group):
            return pl.ds(pl.multiple_of((step * together + group) * LANES, LANES), LANES)

        def head_scores(head):
            group, low = heads[head]
            group_queries = queries_ref[:, columns(group)]
            head_queries = jnp.where(own_lanes(low), group_queries, jnp.zeros_like(group_queries))
            return jnp.dot(
                head_queries, keys_ref[columns(group), :], preferred_element_type=F32
            )

        upcoming = head_scores(0)
        joined = None
        for head, (group, low) in enumerate(heads):
            scores = upcoming
            if head + 1 < len(heads):
                upcoming = head_scores(head + 1)
            row_max = jnp.max(scores, axis=1, keepdims=True)
            probs = jnp.exp2(scores - row_max).astype(BF16)
            sums = jnp.dot(
                probs, values_ref[step * together + group], preferred_element_type=F32
            )
            head_out = sums[:, :LANES] / sums[:, LANES:]
            joined = head_out if low == 0 else jnp.where(own_lanes(low), head_out, joined)
            if low + head_dim == LANES:
                attended_ref[:, columns(group)] = joined.astype(BF16)
        return 0

    lax.fori_loop(0, groups // together, group_step, 0)
    mixed = (
        tokens_ref[...].astype(F32)
        + jnp.dot(attended_ref[...], w_out_ref[...], preferred_element_type=F32)
    ).astype(BF16)
    plane_in = (plain_norm(mixed.astype(F32)) * gain_ref[...]).astype(BF16)
    plane_in_ref[...] = plane_in
    planes_ref[...] = contract(w_plane_ref[...], plane_in, 1, 1).astype(BF16)


def attend_call(images, w_key, w_value, tokens, queries, w_out, norm_gain, w_plane_t, head_dim):
    rows, width = tokens.shape
    channels = w_plane_t.shape[0]
    image_rows = sum(piece.shape[0] for piece in images)
    tile = math.gcd(rows, 768)
    row_block = pl.BlockSpec((tile, width), lambda step: (step, 0))
    return pl.pallas_call(
        functools.partial(attend_kernel, head_dim, len(images)),
        grid=(rows // tile,),
        in_specs=[
            *[whole(piece.shape) for piece in images],
            whole(w_key.shape),
            whole(w_value.shape),
            row_block,
            row_block,
            whole(w_out.shape),
            whole((1, width)),
            whole(w_plane_t.shape),
        ],
        out_specs=[row_block, pl.BlockSpec((channels, tile), lambda step: (0, step))],
        out_shape=[
            jax.ShapeDtypeStruct((rows, width), BF16),
            jax.ShapeDtypeStruct((channels, rows), BF16),
        ],
        scratch_shapes=[
            pltpu.VMEM((width, image_rows), BF16),
            pltpu.VMEM((width // LANES, image_rows, 2 * LANES), BF16),
            pltpu.VMEM((tile, width), BF16),
        ],
        cost_estimate=estimate(4 * rows * width * (image_rows + width // 2), 2 * rows * width),
        compiler_params=params(),
        name="attention_planes",
    )(*images, w_key, w_value, tokens, queries, w_out, norm_gain.reshape(1, width), w_plane_t)


def corners_kernel(grid_side, row_span, index_ref, weight_ref, table_ref):
    index = index_ref[...]
    weights = weight_ref[...].astype(F32)
    plane_size = grid_side * grid_side
    for plane in range(PLANES):
        in_plane = (index >= plane * plane_size) & (index < (plane + 1) * plane_size)
        base = jnp.min(jnp.where(in_plane, index, PLANES * plane_size), axis=0, keepdims=True)
        local = base - plane * plane_size
        first_row = local // grid_side
        band_id = first_row // row_span
        places = [band_id, first_row - band_id * row_span, local - first_row * grid_side]
        picked = [
            jnp.sum(jnp.where(index == base + shift, weights, 0.0), axis=0, keepdims=True)
            for shift in (0, 1, grid_side, grid_side + 1)
        ]
        rows = [place.astype(F32) for place in places] + picked + [jnp.zeros_like(picked[0])]
        table_ref[plane] = jnp.concatenate(rows, axis=0)


def corners_call(index, weights, tokens):
    samples = index.shape[1]
    grid_side = math.isqrt(tokens // PLANES)
    return pl.pallas_call(
        functools.partial(corners_kernel, grid_side, band_span(grid_side)),
        out_shape=jax.ShapeDtypeStruct((PLANES, 8, samples), F32),
        cost_estimate=estimate(1000 * samples, 100 * samples),
        compiler_params=params(16 * MIB),
        name="corners",
    )(index, weights)


def band_span(grid_side):
    return next(span for span in range(7, 0, -1) if (grid_side - 1) % span == 0)


def shifted_left(block, lanes):
    return pltpu.roll(block, block.shape[1] - lanes, 1) if lanes else block


def render_kernel(grid_side, row_span, shares, tile, *refs):
    piece_refs, refs = refs[:shares], refs[shares:]
    (table_ref, target_ref, w1_ref, b1_ref, w2_ref, b2_ref, w3_ref, b3_ref), refs = (
        refs[:8],
        refs[8:],
    )
    colors_ref, even_refs, odd_refs = (
        refs[0],
        refs[1 : 1 + shares // 2],
        refs[1 + shares // 2 : 1 + shares],
    )
    bands_ref, sums_ref, matrix_ref, whole_ref, slope_ref = refs[1 + shares :]
    me = lax.axis_index("seq")
    channels, share = piece_refs[0].shape
    samples = table_ref.shape[-1]
    plane_size = grid_side * grid_side
    band_rows = row_span + 1
    band = band_rows * grid_side
    stride = row_span * grid_side
    bands = (grid_side - 1) // row_span
    rays = tile // STEPS
    whole_rays = target_ref.shape[1]

    def column(row_ref):
        extent = row_ref.shape[1]
        on_diagonal = lax.broadcasted_iota(jnp.int32, (extent, extent), 0) == lax.broadcasted_iota(
            jnp.int32, (extent, extent), 1
        )
        return jnp.sum(jnp.where(on_diagonal, row_ref[...], 0.0), axis=1, keepdims=True)

    bias1, bias2, bias3 = column(b1_ref), column(b2_ref), column(b3_ref)
    earlier = lax.broadcasted_iota(jnp.int32, (STEPS, STEPS), 0)
    later = lax.broadcasted_iota(jnp.int32, (STEPS, STEPS), 1)
    sum_before = jnp.where(earlier < later, 1.0, 0.0)
    sum_behind = jnp.where(earlier > later, 1.0, 0.0)

    for k in range(shares):
        whole_ref[me ^ k] = piece_refs[k][...]
    whole_planes = jnp.concatenate([whole_ref[i] for i in range(shares)], axis=1)
    for plane in range(PLANES):
        for q in range(bands):
            start = plane * plane_size + q * stride
            lead = start % LANES
            extent = band + (LANES if lead else 0)
            piece = whole_planes[:, start - lead : start - lead + extent]
            if lead:
                piece = shifted_left(piece.astype(F32), lead).astype(BF16)
            bands_ref[plane, q * channels : (q + 1) * channels, :] = piece[:, :band]

    def interpolate(part):
        part_samples = pl.ds(pl.multiple_of(part * tile, tile), tile)
        features = jnp.zeros((channels, tile), F32)
        x_ids = lax.broadcasted_iota(jnp.int32, (grid_side, tile), 0).astype(F32)
        for plane in range(PLANES):
            band_id, band_row, first_x, *picked = (
                table_ref[plane, row : row + 1, part_samples] for row in range(7)
            )
            at_first = x_ids == first_x
            at_second = x_ids == first_x + 1.0
            upper = jnp.where(at_first, picked[0], jnp.where(at_second, picked[1], 0.0))
            lower = jnp.where(at_first, picked[2], jnp.where(at_second, picked[3], 0.0))
            upper, lower = upper.astype(BF16), lower.astype(BF16)
            marks = [jnp.where(band_row == r, 1.0, 0.0).astype(BF16) for r in range(row_span)]
            for r in range(band_rows):
                block = upper * marks[r] if r < row_span else None
                if r > 0:
                    below = lower * marks[r - 1]
                    block = below if block is None else block + below
                matrix_ref[plane, r * grid_side : (r + 1) * grid_side, part_samples] = block
            products = jnp.dot(
                bands_ref[plane], matrix_ref[plane, :, part_samples], preferred_element_type=F32
            )
            for q in range(bands):
                features = features + jnp.where(
                    band_id == q, products[q * channels : (q + 1) * channels, :], 0.0
                )
        return features.astype(BF16)

    def shade(part, features):
        pre1 = jnp.dot(w1_ref[...], features, preferred_element_type=F32) + bias1
        gate1 = jax.nn.sigmoid(pre1)
        hidden1 = (pre1 * gate1).astype(BF16)
        pre2 = jnp.dot(w2_ref[...], hidden1, preferred_element_type=F32) + bias2
        gate2 = jax.nn.sigmoid(pre2)
        hidden2 = (pre2 * gate2).astype(BF16)
        decoded = jnp.dot(w3_ref[...], hidden2, preferred_element_type=F32) + bias3

        def by_ray(row):
            return jnp.concatenate(
                [decoded[row : row + 1, i * STEPS : (i + 1) * STEPS] for i in range(rays)], axis=0
            )

        def along_lanes(by_rays):
            return jnp.concatenate([by_rays[i : i + 1, :] for i in range(rays)], axis=1)

        raw_density = by_ray(0)
        density = jnp.maximum(raw_density, 0.0) + jnp.log1p(jnp.exp(-jnp.abs(raw_density)))
        optical = density * DEPTH_STEP
        before = jnp.dot(
            optical, sum_before, preferred_element_type=F32, precision=lax.Precision.HIGHEST
        )
        through = jnp.exp(-before)
        passing = jnp.exp(-optical)
        ray_weight = through * (1.0 - passing)
        own_ray = lax.broadcasted_iota(jnp.int32, (rays, whole_rays), 1) == (
            part * rays + lax.broadcasted_iota(jnp.int32, (rays, whole_rays), 0)
        )
        weight_slope = jnp.zeros((rays, STEPS), F32)
        color_rows = []
        decoded_slopes = []
        for channel in range(3):
            albedo = jax.nn.sigmoid(by_ray(1 + channel))
            color = jnp.sum(ray_weight * albedo, axis=1, keepdims=True)
            color_rows.append(jnp.sum(jnp.where(own_ray, color, 0.0), axis=0, keepdims=True))
            target = target_ref[channel : channel + 1, :]
            residual = color - jnp.sum(jnp.where(own_ray, target, 0.0), axis=1, keepdims=True)
            weight_slope = weight_slope + residual * albedo
            decoded_slopes.append(along_lanes(residual * ray_weight * albedo * (1.0 - albedo)))
        behind = jnp.dot(
            weight_slope * ray_weight,
            sum_behind,
            preferred_element_type=F32,
            precision=lax.Precision.HIGHEST,
        )
        optical_slope = weight_slope * through * passing - behind
        density_slope = optical_slope * DEPTH_STEP * jax.nn.sigmoid(raw_density)
        decoded_slope = jnp.concatenate([along_lanes(density_slope)] + decoded_slopes, axis=0)
        hidden2_slope = contract(w3_ref[...], decoded_slope.astype(BF16), 0, 0).astype(BF16)
        pre2_slope = hidden2_slope.astype(F32) * (gate2 * (1.0 + pre2 * (1.0 - gate2)))
        hidden1_slope = contract(w2_ref[...], pre2_slope.astype(BF16), 0, 0).astype(BF16)
        pre1_slope = hidden1_slope.astype(F32) * (gate1 * (1.0 + pre1 * (1.0 - gate1)))
        slope = contract(w1_ref[...], pre1_slope.astype(BF16), 0, 0).astype(BF16)
        return jnp.concatenate(color_rows, axis=0), slope

    colors_ref[...] = jnp.zeros(colors_ref.shape, F32)

    def render_part(part, _):
        colors, slope = shade(part, interpolate(part))
        colors_ref[...] += colors
        slope_ref[:, pl.ds(pl.multiple_of(part * tile, tile), tile)] = slope
        return 0

    lax.fori_loop(0, samples // tile, render_part, 0)

    def scatter(plane, _):
        slope = slope_ref[...]
        band_id = table_ref[plane, 0:1, :]
        spread = jnp.concatenate(
            [slope * jnp.where(band_id == q, 1.0, 0.0).astype(BF16) for q in range(bands)], axis=0
        )
        sums_ref[plane] = contract(spread, matrix_ref[plane], 1, 1)
        return 0

    lax.fori_loop(0, PLANES, scatter, 0)

    joined = []
    for plane in range(PLANES):
        rows = []
        for kind in range(2):
            parts, reached = [], 0
            for q in range(kind, bands, 2):
                start = q * stride
                lead = start % LANES
                piece = sums_ref[plane, q * channels : (q + 1) * channels, :]
                if lead:
                    piece = jnp.concatenate([piece, jnp.zeros((channels, LANES), F32)], axis=1)
                    piece = pltpu.roll(piece, lead, 1)
                if start - lead > reached:
                    parts.append(jnp.zeros((channels, start - lead - reached), F32))
                parts.append(piece)
                reached = start - lead + piece.shape[1]
            if plane_size > reached:
                parts.append(jnp.zeros((channels, plane_size - reached), F32))
            rows.append(jnp.concatenate(parts, axis=1))
        joined.append((rows[0] + rows[1]).astype(BF16))
    joined = jnp.concatenate(joined, axis=1)
    for i in range(shares):
        whole_ref[i] = joined[:, i * share : (i + 1) * share]
    for k in range(0, shares, 2):
        even_refs[k // 2][...] = whole_ref[me ^ k]
        odd_refs[k // 2][...] = whole_ref[me ^ (k + 1)]


def render_call(pieces, table, target, w1, b1, w2, b2, w3, b3):
    shares = len(pieces)
    channels, share = pieces[0].shape
    samples = table.shape[-1]
    grid_side = math.isqrt(shares * share // PLANES)
    row_span = band_span(grid_side)
    bands = (grid_side - 1) // row_span
    band = (row_span + 1) * grid_side
    tile = math.gcd(samples // STEPS, TILE_RAYS) * STEPS
    row = lambda array: array.reshape(1, -1)
    colors, *grads = pl.pallas_call(
        functools.partial(render_kernel, grid_side, row_span, shares, tile),
        out_shape=[
            jax.ShapeDtypeStruct(target.shape, F32),
            *[jax.ShapeDtypeStruct((channels, share), BF16)] * shares,
        ],
        scratch_shapes=[
            pltpu.VMEM((PLANES, bands * channels, band), BF16),
            pltpu.VMEM((PLANES, bands * channels, band), F32),
            pltpu.VMEM((PLANES, band, samples), BF16),
            pltpu.VMEM((shares, channels, share), BF16),
            pltpu.VMEM((channels, samples), BF16),
        ],
        compiler_params=params(),
        name="render",
    )(*pieces, table, target, w1, row(b1), w2, row(b2), w3, row(b3))
    return colors, grads[: shares // 2], grads[shares // 2 :]


def weight_grad_kernel(count, *refs):
    part_refs, (plane_in_ref, even_ref, odd_ref, grad_ref, chunk_ref) = refs[:count], refs[count:]
    me = lax.axis_index("seq")
    grad = part_refs[0][...].astype(F32)
    for ref in part_refs[1:]:
        grad = grad + ref[...].astype(F32)
    grad = grad.astype(BF16)
    grad_ref[...] = grad
    total = jnp.dot(grad, plane_in_ref[...], preferred_element_type=F32)
    shares, _, columns = chunk_ref.shape
    for i in range(shares):
        chunk_ref[i] = total[:, i * columns : (i + 1) * columns]
    for j in range(shares // 2):
        even_ref[j] = chunk_ref[me ^ (2 * j)]
        odd_ref[j] = chunk_ref[me ^ (2 * j + 1)]


def weight_grad_call(parts, plane_in, shares):
    rows, width = plane_in.shape
    channels = parts[0].shape[0]
    columns = width // shares
    chunks = (shares // 2, channels, columns)
    return pl.pallas_call(
        functools.partial(weight_grad_kernel, len(parts)),
        out_shape=[
            jax.ShapeDtypeStruct(chunks, F32),
            jax.ShapeDtypeStruct(chunks, F32),
            jax.ShapeDtypeStruct((channels, rows), BF16),
        ],
        scratch_shapes=[pltpu.VMEM((shares, channels, columns), F32)],
        compiler_params=pltpu.CompilerParams(vmem_limit_bytes=VMEM_BYTES),
        name="weight_grad",
    )(*parts, plane_in)


def token_grad_kernel(grad_ref, w_plane_ref, token_grad_ref):
    token_grad_ref[...] = contract(grad_ref[...], w_plane_ref[...], 0, 0).astype(BF16)


def token_grad_call(grad, w_plane_t):
    channels, rows = grad.shape
    width = w_plane_t.shape[1]
    tile = math.gcd(rows, 384)
    return pl.pallas_call(
        token_grad_kernel,
        grid=(rows // tile,),
        in_specs=[
            pl.BlockSpec((channels, tile), lambda step: (0, step)),
            whole(w_plane_t.shape),
        ],
        out_specs=pl.BlockSpec((tile, width), lambda step: (step, 0)),
        out_shape=jax.ShapeDtypeStruct((rows, width), BF16),
        cost_estimate=estimate(2 * rows * width * channels, 2 * rows * width),
        compiler_params=params(16 * MIB),
        name="token_grad",
    )(grad, w_plane_t)


def join_kernel(count, *refs):
    chunk_refs, (out_ref, chunks_ref) = refs[:count], refs[count:]
    me = lax.axis_index("seq")
    columns = chunk_refs[0].shape[1]
    for k in range(count):
        chunks_ref[me ^ k] = chunk_refs[k][...]
    for i in range(count):
        out_ref[:, i * columns : (i + 1) * columns] = chunks_ref[i]


def join_call(chunks):
    channels, columns = chunks[0].shape
    return pl.pallas_call(
        functools.partial(join_kernel, len(chunks)),
        out_shape=jax.ShapeDtypeStruct((channels, columns * len(chunks)), F32),
        scratch_shapes=[pltpu.VMEM((len(chunks), channels, columns), F32)],
        name="join_weight_grad",
    )(*chunks)


def body(
    tokens,
    image_tokens,
    norm_gain,
    w_query,
    w_key,
    w_value,
    w_out,
    w_plane,
    dec_w1,
    dec_b1,
    dec_w2,
    dec_b2,
    dec_w3,
    dec_b3,
    corner_idx,
    corner_wts,
    target_color,
):
    own_tokens = tokens[0]
    head_dim = own_tokens.shape[1] // HEADS
    query_scale = math.log2(math.e) / math.sqrt(head_dim)
    shares = lax.axis_size("seq")
    rows_here = own_tokens.shape[0]
    far_images = from_chips(image_tokens[0])
    images = with_other_core([image_tokens[0]])
    queries = query_call(own_tokens, w_query, query_scale)
    far_images, queries = lax.optimization_barrier((far_images, queries))
    images = images + with_other_core(far_images)
    w_plane_t = w_plane.T
    plane_in, planes = attend_call(
        images, w_key, w_value, own_tokens, queries, w_out, norm_gain, w_plane_t, head_dim
    )
    far_planes = from_chips(planes)
    planes = with_other_core([planes])
    table = corners_call(corner_idx[0], corner_wts[0], shares * rows_here)
    far_planes, table = lax.optimization_barrier((far_planes, table))
    colors, kept, passed = render_call(
        planes + with_other_core(far_planes),
        table,
        target_color[0],
        dec_w1,
        dec_b1,
        dec_w2,
        dec_b2,
        dec_w3,
        dec_b3,
    )
    parts = []
    for j in reversed(range(shares // 2)):
        pair = (kept[j].astype(F32) + swap(passed[j], "seq", 1).astype(F32)).astype(BF16)
        parts.append(swap(pair, "seq", 2 * j) if j else pair)
    kept, passed, grad = weight_grad_call(parts, plane_in, shares)
    pairs = kept + swap(passed, "seq", 1)
    chunk = pairs[0]
    for j in range(1, shares // 2):
        chunk = chunk + swap(pairs[j], "seq", 2 * j)
    others = [swap(chunk, "dp", k) for k in range(1, lax.axis_size("dp"))]
    token_grad = token_grad_call(grad, w_plane_t)
    others, token_grad = lax.optimization_barrier((others, token_grad))
    scenes = sum(others, chunk)
    weight_grad = join_call(gather_scene(scenes)).T
    return (colors[None], token_grad[None], weight_grad)


def solution(mesh):
    in_specs = (
        P("dp", "seq", None),
        P("dp", "seq", None),
        P(),
        P(),
        P(),
        P(),
        P(),
        P(),
        P(),
        P(),
        P(),
        P(),
        P(),
        P(),
        P("dp", None, "seq"),
        P("dp", None, "seq"),
        P("dp", None, "seq"),
    )
    out_specs = (P("dp", None, "seq"), P("dp", "seq", None), P())
    return jax.shard_map(body, mesh=mesh, in_specs=in_specs, out_specs=out_specs, check_vma=False)
```

profile of v0, /device:TPU:1, one launch (start us, length us, event | category | flops | bytes accessed | tf_op | source)
XLA Modules:
  0.0 159.4 jit_solution(6571285541411122636)
XLA Ops:
  0.6 2.1 %collective-permute-start.1 = (bf16[128,768]{1,0:T(8,128)(2,1)}, bf16[128,768]{1,0:T(8,128)(2,1)S(1)}, u32[]{:S(2)}, u32[]{:S(2)}) collective-permute-start(bf16[128,768]{1,0:T(8,128)(2,1)} %bitcast.44), channel_id=1, source_target_pairs={{0,2},{1,3},{2,0},{3,1},{4,6},{5,7},{6,4},{7,5},{8,10},{9,11},{10,... | collective-permute-start | bytes 589832 | tf_op jit(solution)/shard_map/ppermute | solution.py:50
  5.2 1.9 %copy-done.4 = bf16[1,1536,1024]{2,1,0:T(8,128)(2,1)S(1)} copy-done((bf16[1,1536,1024]{2,1,0:T(8,128)(2,1)S(1)}, bf16[1,1536,1024]{2,1,0:T(8,128)(2,1)}, u32[]{:S(2)}) %copy-start.4) | copy-done | bytes 3145752
  7.1 1.6 copy-done.5
  8.7 5.1 %queries.1.refs_11_ = bf16[1536,1024]{1,0:T(8,128)(2,1)S(1)} custom-call(bf16[1536,1024]{1,0:T(8,128)(2,1)S(1)} %bitcast.36, bf16[1024,1024]{1,0:T(8,128)(2,1)S(1)} %copy-done.5), custom_call_target="tpu_custom_call" | custom-call | flops 3221225472 | bytes 6291456 | tf_op jit(solution)/shard_map/queries/pallas_call | solution.py:86
  13.8 1.7 %copy-done.6 = bf16[1536,1024]{1,0:T(8,128)(2,1)} copy-done((bf16[1536,1024]{1,0:T(8,128)(2,1)}, bf16[1536,1024]{1,0:T(8,128)(2,1)S(1)}, u32[]{:S(2)}) %copy-start.6) | copy-done | bytes 3145752
  18.3 44.4 %attention_planes.1 = (bf16[1536,1024]{1,0:T(8,128)(2,1)}, bf16[80,1536]{1,0:T(8,128)(2,1)}) custom-call(bf16[128,768]{1,0:T(8,128)(2,1)} %bitcast.48, bf16[128,768]{1,0:T(8,128)(2,1)} %copy-done.31, bf16[128,768]{1,0:T(8,128)(2,1)} %copy-done.28, bf16[128,768]{1,0:T(8,128)(2,1)} %copy-done.32, bf16[128,768]{1,0:T(8,128)(2,1)} %copy-done.29, ...), custom_call_target="tpu_custom_call" | custom-call | flops 9663676416 | bytes 3145728 | tf_op jit(solution)/shard_map/attention_planes/pallas_call | solution.py:168
  62.7 2.7 %collective-permute-start.10 = (bf16[80,1536]{1,0:T(8,128)(2,1)}, bf16[80,1536]{1,0:T(8,128)(2,1)S(1)}, u32[]{:S(2)}, u32[]{:S(2)}) collective-permute-start(bf16[80,1536]{1,0:T(8,128)(2,1)} %get-tuple-element.33.refs_0_), channel_id=1, source_target_pairs={{0,6},{1,7},{2,4},{3,5},{4,2},{5,3},{6,0},{7,1},{8,14},{9,15},{10,... | collective-permute-start | bytes 737288 | tf_op jit(solution)/shard_map/ppermute | solution.py:50
  65.9 1.6 %corners.1.refs_8_ = f32[3,8,4096]{2,1,0:T(8,128)S(1)} custom-call(s32[12,4096]{1,0:T(8,128)S(1)} %bitcast.31, bf16[12,4096]{1,0:T(8,128)(2,1)S(1)} %bitcast.34), custom_call_target="tpu_custom_call" | custom-call | flops 4096000 | bytes 409600 | tf_op jit(solution)/shard_map/corners/pallas_call | solution.py:219
  69.0 2.7 %collective-permute-done.10.refs_6_ = bf16[80,1536]{1,0:T(8,128)(2,1)S(1)} collective-permute-done((bf16[80,1536]{1,0:T(8,128)(2,1)}, bf16[80,1536]{1,0:T(8,128)(2,1)S(1)}, u32[]{:S(2)}, u32[]{:S(2)}) %collective-permute-start.10) | collective-permute-done | bytes 245792 | tf_op jit(solution)/shard_map/ppermute | solution.py:50
  71.8 5.2 %collective-permute-done.8.refs_2_ = bf16[80,1536]{1,0:T(8,128)(2,1)S(1)} collective-permute-done((bf16[80,1536]{1,0:T(8,128)(2,1)}, bf16[80,1536]{1,0:T(8,128)(2,1)S(1)}, u32[]{:S(2)}, u32[]{:S(2)}) %collective-permute-start.8) | collective-permute-done | bytes 245792 | tf_op jit(solution)/shard_map/ppermute | solution.py:50
  80.7 25.1 %render.1 = (f32[3,32]{1,0:T(4,128)}, bf16[80,1536]{1,0:T(8,128)(2,1)}, bf16[80,1536]{1,0:T(8,128)(2,1)}, bf16[80,1536]{1,0:T(8,128)(2,1)}, bf16[80,1536]{1,0:T(...) custom-call(bf16[80,1536]{1,0:T(8,128)(2,1)} %get-tuple-element.33.r, ...), custom_call_target="tpu_custom_call" | custom-call | tf_op jit(solution)/shard_map/render/pallas_call | solution.py:429
  113.5 1.7 %add_convert_fusion.refs_3_ = bf16[80,1536]{1,0:T(8,128)(2,1)} fusion(bf16[80,1536]{1,0:T(8,128)(2,1)S(1)} %collective-permute-done.20, bf16[80,1536]{1,0:T(8,128)(2,1)} %get-tuple-element.45), kind=kLoop, calls=%fused_computation | loop fusion | flops 491520 | bytes 737280 | tf_op jit(solution)/shard_map/convert_element_type | solution.py:576
  115.9 7.2 %collective-permute-done.17.refs_1_ = bf16[80,1536]{1,0:T(8,128)(2,1)S(1)} collective-permute-done((bf16[80,1536]{1,0:T(8,128)(2,1)S(1)}, bf16[80,1536]{1,0:T(8,128)(2,1)S(1)}, u32[]{:S(2)}, u32[]{:S(2)}) %collective-permute-start.17) | collective-permute-done | bytes 245792 | tf_op jit(solution)/shard_map/ppermute | solution.py:50
  123.8 3.9 %weight_grad.1 = (f32[4,80,128]{2,1,0:T(8,128)}, f32[4,80,128]{2,1,0:T(8,128)}, bf16[80,1536]{1,0:T(8,128)(2,1)}) custom-call(bf16[80,1536]{1,0:T(8,128)(2,1)} %copy-done.9, bf16[80,1536]{1,0:T(8,128)(2,1)} %copy-done.8, bf16[80,1536]{1,0:T(8,128)(2,1)} %copy-done.7, bf16[80,1536]{1,0:T(8,128)(2,1)} %add_convert_fusion.refs_3_, ...), custom_call_target="tpu_custom_call" | custom-call | tf_op jit(solution)/shard_map/weight_grad/pallas_call | solution.py:470
  127.7 1.5 collective-permute-start.21
  132.8 1.3 collective-permute-start.24
  134.6 2.0 %collective-permute-done.24 = f32[80,128]{1,0:T(8,128)S(1)} collective-permute-done((f32[80,128]{1,0:T(8,128)S(1)}, f32[80,128]{1,0:T(8,128)S(1)}, u32[]{:S(2)}, u32[]{:S(2)}) %collective-permute-start.24) | collective-permute-done | bytes 40992 | tf_op jit(solution)/shard_map/ppermute | solution.py:50
  136.6 1.3 collective-permute-start.25
  137.9 2.3 %collective-permute-start.26 = (f32[80,128]{1,0:T(8,128)S(1)}, f32[80,128]{1,0:T(8,128)S(1)}, u32[]{:S(2)}, u32[]{:S(2)}) collective-permute-start(f32[80,128]{1,0:T(8,128)S(1)} %fusion.2), channel_id=1, source_target_pairs={{0,16},{8,24},{16,0},{24,8},{1,17},{9,25},{17,1},{25,9},{2,18},{10... | collective-permute-start | bytes 122888 | tf_op jit(solution)/shard_map/ppermute | solution.py:50
  141.2 3.0 %token_grad.1 = bf16[1536,1024]{1,0:T(8,128)(2,1)} custom-call(bf16[80,1536]{1,0:T(8,128)(2,1)S(1)} %copy-done.1, bf16[80,1024]{1,0:T(8,128)(2,1)S(1)} %bitcast.33), custom_call_target="tpu_custom_call" | custom-call | flops 251658240 | bytes 3145728 | tf_op jit(solution)/shard_map/token_grad/pallas_call | solution.py:491
  147.8 4.5 %collective-permute-start.28 = (f32[80,128]{1,0:T(8,128)S(1)}, f32[80,128]{1,0:T(8,128)S(1)}, u32[]{:S(2)}, u32[]{:S(2)}) collective-permute-start(f32[80,128]{1,0:T(8,128)S(1)} %add_add_fusion.refs_0_), channel_id=1, source_target_pairs={{0,1},{1,0},{2,3},{3,2},{4,5},{5,4},{6,7},{7,6},{8,9},{9,8},{10,11... | collective-permute-start | bytes 122888 | tf_op jit(solution)/shard_map/ppermute | solution.py:50
  152.8 1.5 collective-permute-start.32
  154.3 1.6 collective-permute-start.34
  157.7 1.7 %join_weight_grad.1 = f32[80,1024]{1,0:T(8,128)} custom-call(f32[80,128]{1,0:T(8,128)} %copy-done.18, f32[80,128]{1,0:T(8,128)} %copy-done.22, f32[80,128]{1,0:T(8,128)} %copy-done.19, f32[80,128]{1,0:T(8,128)} %copy-done.23, f32[80,128]{1,0:T(8,128)} %copy-done.20, f32[80,128]{1,0:T(8,128)} %copy-done.24, f32[80,128]{1,0:T(8,128)} %copy-done.21, ...), custom_call_target="tpu_custom_call" | custom-call | tf_op jit(solution)/shard_map/join_weight_grad/pallas_call | solution.py:518
  (134 shorter events, 31.0 us)
Async XLA Ops:
  0.6 14.8 %collective-permute-start.1 = (bf16[128,768]{1,0:T(8,128)(2,1)}, bf16[128,768]{1,0:T(8,128)(2,1)S(1)}, u32[]{:S(2)}, u32[]{:S(2)}) collective-permute-start(bf16[128,768]{1,0:T(8,128)(2,1)} %bitcast.44), channel_id=1, source_target_pairs={{0,2},{1,3},{2,0},{3,1},{4,6},{5,7},{6,4},{7,5},{8,10},{9,11},{10,... | collective-permute-start | bytes 589832 | tf_op jit(solution)/shard_map/ppermute | solution.py:50
  2.7 12.7 %collective-permute-start.2 = (bf16[128,768]{1,0:T(8,128)(2,1)}, bf16[128,768]{1,0:T(8,128)(2,1)S(1)}, u32[]{:S(2)}, u32[]{:S(2)}) collective-permute-start(bf16[128,768]{1,0:T(8,128)(2,1)} %bitcast.45), channel_id=1, source_target_pairs={{0,4},{1,5},{2,6},{3,7},{4,0},{5,1},{6,2},{7,3},{8,12},{9,13},{10,... | collective-permute-start | bytes 589832 | tf_op jit(solution)/shard_map/ppermute | solution.py:50
  4.0 11.5 %collective-permute-start.3 = (bf16[128,768]{1,0:T(8,128)(2,1)}, bf16[128,768]{1,0:T(8,128)(2,1)S(1)}, u32[]{:S(2)}, u32[]{:S(2)}) collective-permute-start(bf16[128,768]{1,0:T(8,128)(2,1)} %bitcast.46), channel_id=1, source_target_pairs={{0,6},{1,7},{2,4},{3,5},{4,2},{5,3},{6,0},{7,1},{8,14},{9,15},{10,... | collective-permute-start | bytes 589832 | tf_op jit(solution)/shard_map/ppermute | solution.py:50
  4.0 12.2 %collective-permute-start = (bf16[128,768]{1,0:T(8,128)(2,1)}, bf16[128,768]{1,0:T(8,128)(2,1)S(1)}, u32[]{:S(2)}, u32[]{:S(2)}) collective-permute-start(bf16[128,768]{1,0:T(8,128)(2,1)} %bitcast.47), channel_id=1, source_target_pairs={{0,1},{1,0},{2,3},{3,2},{4,5},{5,4},{6,7},{7,6},{8,9},{9,8},{10,11... | collective-permute-start | bytes 589832 | tf_op jit(solution)/shard_map/ppermute | solution.py:50
  62.7 9.1 %collective-permute-start.10 = (bf16[80,1536]{1,0:T(8,128)(2,1)}, bf16[80,1536]{1,0:T(8,128)(2,1)S(1)}, u32[]{:S(2)}, u32[]{:S(2)}) collective-permute-start(bf16[80,1536]{1,0:T(8,128)(2,1)} %get-tuple-element.33.refs_0_), channel_id=1, source_target_pairs={{0,6},{1,7},{2,4},{3,5},{4,2},{5,3},{6,0},{7,1},{8,14},{9,15},{10,... | collective-permute-start | bytes 737288 | tf_op jit(solution)/shard_map/ppermute | solution.py:50
  65.4 11.6 %collective-permute-start.8 = (bf16[80,1536]{1,0:T(8,128)(2,1)}, bf16[80,1536]{1,0:T(8,128)(2,1)S(1)}, u32[]{:S(2)}, u32[]{:S(2)}) collective-permute-start(bf16[80,1536]{1,0:T(8,128)(2,1)} %get-tuple-element.33.refs_0_), channel_id=1, source_target_pairs={{0,2},{1,3},{2,0},{3,1},{4,6},{5,7},{6,4},{7,5},{8,10},{9,11},{10,... | collective-permute-start | bytes 737288 | tf_op jit(solution)/shard_map/ppermute | solution.py:50
  65.6 11.6 %collective-permute-start.9 = (bf16[80,1536]{1,0:T(8,128)(2,1)}, bf16[80,1536]{1,0:T(8,128)(2,1)S(1)}, u32[]{:S(2)}, u32[]{:S(2)}) collective-permute-start(bf16[80,1536]{1,0:T(8,128)(2,1)} %get-tuple-element.33.refs_0_), channel_id=1, source_target_pairs={{0,4},{1,5},{2,6},{3,7},{4,0},{5,1},{6,2},{7,3},{8,12},{9,13},{10,... | collective-permute-start | bytes 737288 | tf_op jit(solution)/shard_map/ppermute | solution.py:50
  68.3 11.0 %collective-permute-start.7 = (bf16[80,1536]{1,0:T(8,128)(2,1)}, bf16[80,1536]{1,0:T(8,128)(2,1)S(1)}, u32[]{:S(2)}, u32[]{:S(2)}) collective-permute-start(bf16[80,1536]{1,0:T(8,128)(2,1)} %get-tuple-element.33.refs_0_), channel_id=1, source_target_pairs={{0,1},{1,0},{2,3},{3,2},{4,5},{5,4},{6,7},{7,6},{8,9},{9,8},{10,11... | collective-permute-start | bytes 737288 | tf_op jit(solution)/shard_map/ppermute | solution.py:50
  106.2 7.3 %collective-permute-start.20 = (bf16[80,1536]{1,0:T(8,128)(2,1)}, bf16[80,1536]{1,0:T(8,128)(2,1)S(1)}, u32[]{:S(2)}, u32[]{:S(2)}) collective-permute-start(bf16[80,1536]{1,0:T(8,128)(2,1)} %get-tuple-element.46), channel_id=1, source_target_pairs={{0,1},{1,0},{2,3},{3,2},{4,5},{5,4},{6,7},{7,6},{8,9},{9,8},{10,11... | collective-permute-start | bytes 737288 | tf_op jit(solution)/shard_map/ppermute | solution.py:50
  106.4 3.5 %collective-permute-start.16 = (bf16[80,1536]{1,0:T(8,128)(2,1)}, bf16[80,1536]{1,0:T(8,128)(2,1)S(1)}, u32[]{:S(2)}, u32[]{:S(2)}) collective-permute-start(bf16[80,1536]{1,0:T(8,128)(2,1)} %get-tuple-element.42), channel_id=1, source_target_pairs={{0,1},{1,0},{2,3},{3,2},{4,5},{5,4},{6,7},{7,6},{8,9},{9,8},{10,11... | collective-permute-start | bytes 737288 | tf_op jit(solution)/shard_map/ppermute | solution.py:50
  106.7 5.3 %collective-permute-start.14 = (bf16[80,1536]{1,0:T(8,128)(2,1)}, bf16[80,1536]{1,0:T(8,128)(2,1)S(1)}, u32[]{:S(2)}, u32[]{:S(2)}) collective-permute-start(bf16[80,1536]{1,0:T(8,128)(2,1)} %get-tuple-element.40), channel_id=1, source_target_pairs={{0,1},{1,0},{2,3},{3,2},{4,5},{5,4},{6,7},{7,6},{8,9},{9,8},{10,11... | collective-permute-start | bytes 737288 | tf_op jit(solution)/shard_map/ppermute | solution.py:50
  108.6 7.3 %collective-permute-start.19 = (bf16[80,1536]{1,0:T(8,128)(2,1)S(1)}, bf16[80,1536]{1,0:T(8,128)(2,1)S(1)}, u32[]{:S(2)}, u32[]{:S(2)}) collective-permute-start(bf16[80,1536]{1,0:T(8,128)(2,1)S(1)} %add_convert_fusion.1), channel_id=1, source_target_pairs={{0,2},{1,3},{2,0},{3,1},{4,6},{5,7},{6,4},{7,5},{8,10},{9,11},{10,... | collective-permute-start | bytes 737288 | tf_op jit(solution)/shard_map/ppermute | solution.py:50
  110.9 12.2 %collective-permute-start.17 = (bf16[80,1536]{1,0:T(8,128)(2,1)S(1)}, bf16[80,1536]{1,0:T(8,128)(2,1)S(1)}, u32[]{:S(2)}, u32[]{:S(2)}) collective-permute-start(bf16[80,1536]{1,0:T(8,128)(2,1)S(1)} %add_convert_fusion.2), channel_id=1, source_target_pairs={{0,4},{1,5},{2,6},{3,7},{4,0},{5,1},{6,2},{7,3},{8,12},{9,13},{10,... | collective-permute-start | bytes 737288 | tf_op jit(solution)/shard_map/ppermute | solution.py:50
  113.1 10.0 %collective-permute-start.15 = (bf16[80,1536]{1,0:T(8,128)(2,1)S(1)}, bf16[80,1536]{1,0:T(8,128)(2,1)S(1)}, u32[]{:S(2)}, u32[]{:S(2)}) collective-permute-start(bf16[80,1536]{1,0:T(8,128)(2,1)S(1)} %add_convert_fusion.3), channel_id=1, source_target_pairs={{0,6},{1,7},{2,4},{3,5},{4,2},{5,3},{6,0},{7,1},{8,14},{9,15},{10,... | collective-permute-start | bytes 737288 | tf_op jit(solution)/shard_map/ppermute | solution.py:50
  132.8 3.8 %collective-permute-start.24 = (f32[80,128]{1,0:T(8,128)S(1)}, f32[80,128]{1,0:T(8,128)S(1)}, u32[]{:S(2)}, u32[]{:S(2)}) collective-permute-start(f32[80,128]{1,0:T(8,128)S(1)} %get-tuple-element.59), channel_id=1, source_target_pairs={{0,6},{1,7},{2,4},{3,5},{4,2},{5,3},{6,0},{7,1},{8,14},{9,15},{10,... | collective-permute-start | bytes 122888 | tf_op jit(solution)/shard_map/ppermute | solution.py:50
  136.6 7.6 %collective-permute-start.25 = (f32[80,128]{1,0:T(8,128)S(1)}, f32[80,128]{1,0:T(8,128)S(1)}, u32[]{:S(2)}, u32[]{:S(2)}) collective-permute-start(f32[80,128]{1,0:T(8,128)S(1)} %fusion.2), channel_id=1, source_target_pairs={{0,8},{8,0},{16,24},{24,16},{1,9},{9,1},{17,25},{25,17},{2,10},{10... | collective-permute-start | bytes 122888 | tf_op jit(solution)/shard_map/ppermute | solution.py:50
  137.9 6.2 %collective-permute-start.26 = (f32[80,128]{1,0:T(8,128)S(1)}, f32[80,128]{1,0:T(8,128)S(1)}, u32[]{:S(2)}, u32[]{:S(2)}) collective-permute-start(f32[80,128]{1,0:T(8,128)S(1)} %fusion.2), channel_id=1, source_target_pairs={{0,16},{8,24},{16,0},{24,8},{1,17},{9,25},{17,1},{25,9},{2,18},{10... | collective-permute-start | bytes 122888 | tf_op jit(solution)/shard_map/ppermute | solution.py:50
  140.2 4.8 %collective-permute-start.27 = (f32[80,128]{1,0:T(8,128)S(1)}, f32[80,128]{1,0:T(8,128)S(1)}, u32[]{:S(2)}, u32[]{:S(2)}) collective-permute-start(f32[80,128]{1,0:T(8,128)S(1)} %fusion.2), channel_id=1, source_target_pairs={{0,24},{8,16},{16,8},{24,0},{1,25},{9,17},{17,9},{25,1},{2,26},{10... | collective-permute-start | bytes 122888 | tf_op jit(solution)/shard_map/ppermute | solution.py:50
  145.0 7.2 %collective-permute-start.29 = (f32[80,128]{1,0:T(8,128)S(1)}, f32[80,128]{1,0:T(8,128)S(1)}, u32[]{:S(2)}, u32[]{:S(2)}) collective-permute-start(f32[80,128]{1,0:T(8,128)S(1)} %add_add_fusion.refs_0_), channel_id=1, source_target_pairs={{0,2},{1,3},{2,0},{3,1},{4,6},{5,7},{6,4},{7,5},{8,10},{9,11},{10,... | collective-permute-start | bytes 122888 | tf_op jit(solution)/shard_map/ppermute | solution.py:50
  146.3 6.4 %collective-permute-start.31 = (f32[80,128]{1,0:T(8,128)S(1)}, f32[80,128]{1,0:T(8,128)S(1)}, u32[]{:S(2)}, u32[]{:S(2)}) collective-permute-start(f32[80,128]{1,0:T(8,128)S(1)} %add_add_fusion.refs_0_), channel_id=1, source_target_pairs={{0,4},{1,5},{2,6},{3,7},{4,0},{5,1},{6,2},{7,3},{8,12},{9,13},{10,... | collective-permute-start | bytes 122888 | tf_op jit(solution)/shard_map/ppermute | solution.py:50
  146.7 7.5 %collective-permute-start.33 = (f32[80,128]{1,0:T(8,128)S(1)}, f32[80,128]{1,0:T(8,128)S(1)}, u32[]{:S(2)}, u32[]{:S(2)}) collective-permute-start(f32[80,128]{1,0:T(8,128)S(1)} %add_add_fusion.refs_0_), channel_id=1, source_target_pairs={{0,6},{1,7},{2,4},{3,5},{4,2},{5,3},{6,0},{7,1},{8,14},{9,15},{10,... | collective-permute-start | bytes 122888 | tf_op jit(solution)/shard_map/ppermute | solution.py:50
  147.8 8.6 %collective-permute-start.28 = (f32[80,128]{1,0:T(8,128)S(1)}, f32[80,128]{1,0:T(8,128)S(1)}, u32[]{:S(2)}, u32[]{:S(2)}) collective-permute-start(f32[80,128]{1,0:T(8,128)S(1)} %add_add_fusion.refs_0_), channel_id=1, source_target_pairs={{0,1},{1,0},{2,3},{3,2},{4,5},{5,4},{6,7},{7,6},{8,9},{9,8},{10,11... | collective-permute-start | bytes 122888 | tf_op jit(solution)/shard_map/ppermute | solution.py:50
  152.3 4.1 %collective-permute-start.30 = (f32[80,128]{1,0:T(8,128)S(1)}, f32[80,128]{1,0:T(8,128)S(1)}, u32[]{:S(2)}, u32[]{:S(2)}) collective-permute-start(f32[80,128]{1,0:T(8,128)S(1)} %collective-permute-done.29.refs_2_), channel_id=1, source_target_pairs={{0,1},{1,0},{2,3},{3,2},{4,5},{5,4},{6,7},{7,6},{8,9},{9,8},{10,11... | collective-permute-start | bytes 122888 | tf_op jit(solution)/shard_map/ppermute | solution.py:50
  152.8 3.6 %collective-permute-start.32 = (f32[80,128]{1,0:T(8,128)S(1)}, f32[80,128]{1,0:T(8,128)S(1)}, u32[]{:S(2)}, u32[]{:S(2)}) collective-permute-start(f32[80,128]{1,0:T(8,128)S(1)} %collective-permute-done.31.refs_4_), channel_id=1, source_target_pairs={{0,1},{1,0},{2,3},{3,2},{4,5},{5,4},{6,7},{7,6},{8,9},{9,8},{10,11... | collective-permute-start | bytes 122888 | tf_op jit(solution)/shard_map/ppermute | solution.py:50
  (46 other events, 301.6 us)
where the time goes:
time: 160 us; the launch traced here: 159 us
  Pallas kernels  84.8 us (53%)
  starting transfers between devices  33 us (21%)
  waiting for transfers between devices  23.8 us (15%)
  local copies, waits for them, and re-layouts  11.3 us (7%)
  other arithmetic  5.73 us (4%)
    pallas_call x1, Pallas kernels, attend_call(): pl.pallas_call(functools.partial(attend_kernel, head_dim, len(images)), g...  44.4 us
    ppermute x35, starting transfers between devices, swap(): return lax.ppermute(array, axis, pairs)  33 us
    pallas_call x1, Pallas kernels, render_call(): pl.pallas_call(functools.partial(render_kernel, grid_side, row_span, shar...  25.1 us
    ppermute x35, waiting for transfers between devices, swap(): return lax.ppermute(array, axis, pairs)  23.8 us
    unnamed x73, local copies, waits for them, and re-layouts  11.2 us
    pallas_call x1, Pallas kernels, query_call(): pl.pallas_call(functools.partial(query_kernel, query_scale), grid=(rows /...  5.08 us
    convert_element_type x4, other arithmetic, body(): (kept[j].astype(F32) + swap(passed[j], 'seq', 1).astype(F32)).astype(BF16)  4.76 us
    pallas_call x1, Pallas kernels, weight_grad_call(): pl.pallas_call(functools.partial(weight_grad_kernel, len(parts)), out_sha...  3.87 us
  transfers between devices with their start and end apart: 35, of which 17 were waited for; matrix products, arithmetic and copies ran while one was open for 4% of the time, Pallas kernels for 6%

commit v1 on v0

--- a/solution.py
+++ b/solution.py
@@ -13,12 +13,12 @@
 PLANES = 3
 LANES = 128
 TILE_RAYS = 32
-TOGETHER = 4
+TOGETHER = 8
 
 NORM_EPS = 1e-05
 DEPTH_STEP = 0.02
 MIB = 1024 * 1024
-VMEM_BYTES = 56 * MIB
+VMEM_BYTES = 60 * MIB
 
 F32 = jnp.float32
 BF16 = jnp.bfloat16
@@ -90,7 +90,7 @@
         out_specs=pl.BlockSpec((tile, width), lambda step: (step, 0)),
         out_shape=jax.ShapeDtypeStruct((rows, width), BF16),
         cost_estimate=estimate(2 * rows * width * width, 4 * rows * width),
-        compiler_params=params(32 * MIB),
+        compiler_params=params(),
         name="queries",
     )(tokens, w_query)
 
@@ -163,7 +163,7 @@
     rows, width = tokens.shape
     channels = w_plane_t.shape[0]
     image_rows = sum(piece.shape[0] for piece in images)
-    tile = math.gcd(rows, 768)
+    tile = math.gcd(rows, 384)
     row_block = pl.BlockSpec((tile, width), lambda step: (step, 0))
     return pl.pallas_call(
         functools.partial(attend_kernel, head_dim, len(images)),
@@ -194,7 +194,10 @@
     )(*images, w_key, w_value, tokens, queries, w_out, norm_gain.reshape(1, width), w_plane_t)
 
 
-def corners_kernel(grid_side, row_span, index_ref, weight_ref, table_ref):
+def corners_kernel(
+    grid_side, row_span, index_ref, weight_ref, target_ref, table_ref, target_out_ref
+):
+    target_out_ref[...] = target_ref[...]
     index = index_ref[...]
     weights = weight_ref[...].astype(F32)
     plane_size = grid_side * grid_side
@@ -213,16 +216,19 @@
         table_ref[plane] = jnp.concatenate(rows, axis=0)
 
 
-def corners_call(index, weights, tokens):
+def corners_call(index, weights, target, tokens):
     samples = index.shape[1]
     grid_side = math.isqrt(tokens // PLANES)
     return pl.pallas_call(
         functools.partial(corners_kernel, grid_side, band_span(grid_side)),
-        out_shape=jax.ShapeDtypeStruct((PLANES, 8, samples), F32),
+        out_shape=[
+            jax.ShapeDtypeStruct((PLANES, 8, samples), F32),
+            jax.ShapeDtypeStruct(target.shape, F32),
+        ],
         cost_estimate=estimate(1000 * samples, 100 * samples),
         compiler_params=params(16 * MIB),
         name="corners",
-    )(index, weights)
+    )(index, weights, target)
 
 
 def band_span(grid_side):
@@ -446,20 +452,33 @@
 
 
 def weight_grad_kernel(count, *refs):
-    part_refs, (plane_in_ref, even_ref, odd_ref, grad_ref, chunk_ref) = refs[:count], refs[count:]
-    me = lax.axis_index("seq")
+    part_refs, refs = refs[:count], refs[count:]
+    plane_in_ref, even_ref, odd_ref, grad_ref, total_ref, chunk_ref = refs
+    step = pl.program_id(0)
     grad = part_refs[0][...].astype(F32)
     for ref in part_refs[1:]:
         grad = grad + ref[...].astype(F32)
     grad = grad.astype(BF16)
     grad_ref[...] = grad
-    total = jnp.dot(grad, plane_in_ref[...], preferred_element_type=F32)
-    shares, _, columns = chunk_ref.shape
-    for i in range(shares):
-        chunk_ref[i] = total[:, i * columns : (i + 1) * columns]
-    for j in range(shares // 2):
-        even_ref[j] = chunk_ref[me ^ (2 * j)]
-        odd_ref[j] = chunk_ref[me ^ (2 * j + 1)]
+    product = jnp.dot(grad, plane_in_ref[...], preferred_element_type=F32)
+
+    @pl.when(step == 0)
+    def begin():
+        total_ref[...] = product
+
+    @pl.when(step > 0)
+    def add():
+        total_ref[...] += product
+
+    @pl.when(step == pl.num_programs(0) - 1)
+    def cut():
+        me = lax.axis_index("seq")
+        shares, _, columns = chunk_ref.shape
+        for i in range(shares):
+            chunk_ref[i] = total_ref[:, i * columns : (i + 1) * columns]
+        for j in range(shares // 2):
+            even_ref[j] = chunk_ref[me ^ (2 * j)]
+            odd_ref[j] = chunk_ref[me ^ (2 * j + 1)]
 
 
 def weight_grad_call(parts, plane_in, shares):
@@ -467,15 +486,26 @@
     channels = parts[0].shape[0]
     columns = width // shares
     chunks = (shares // 2, channels, columns)
+    tile = math.gcd(rows, 768)
+    part_block = pl.BlockSpec((channels, tile), lambda step: (0, step))
     return pl.pallas_call(
         functools.partial(weight_grad_kernel, len(parts)),
+        grid=(rows // tile,),
+        in_specs=[
+            *[part_block] * len(parts),
+            pl.BlockSpec((tile, width), lambda step: (step, 0)),
+        ],
+        out_specs=[kept(chunks), kept(chunks), part_block],
         out_shape=[
             jax.ShapeDtypeStruct(chunks, F32),
             jax.ShapeDtypeStruct(chunks, F32),
             jax.ShapeDtypeStruct((channels, rows), BF16),
         ],
-        scratch_shapes=[pltpu.VMEM((shares, channels, columns), F32)],
-        compiler_params=pltpu.CompilerParams(vmem_limit_bytes=VMEM_BYTES),
+        scratch_shapes=[
+            pltpu.VMEM((channels, width), F32),
+            pltpu.VMEM((shares, channels, columns), F32),
+        ],
+        compiler_params=params(),
         name="weight_grad",
     )(*parts, plane_in)
 
@@ -519,6 +549,7 @@
         functools.partial(join_kernel, len(chunks)),
         out_shape=jax.ShapeDtypeStruct((channels, columns * len(chunks)), F32),
         scratch_shapes=[pltpu.VMEM((len(chunks), channels, columns), F32)],
+        compiler_params=params(),
         name="join_weight_grad",
     )(*chunks)
 
@@ -558,12 +589,14 @@
     )
     far_planes = from_chips(planes)
     planes = with_other_core([planes])
-    table = corners_call(corner_idx[0], corner_wts[0], shares * rows_here)
-    far_planes, table = lax.optimization_barrier((far_planes, table))
+    table, target = corners_call(
+        corner_idx[0], corner_wts[0], target_color[0], shares * rows_here
+    )
+    far_planes, table, target = lax.optimization_barrier((far_planes, table, target))
     colors, kept, passed = render_call(
         planes + with_other_core(far_planes),
         table,
-        target_color[0],
+        target,
         dec_w1,
         dec_b1,
         dec_w2,

time: 160 us -> 155 us (0.969)
  local copies, waits for them, and re-layouts: 11.3 us -> 6.03 us
    unnamed x73 -> x69, local copies, waits for them, and re-layouts: 11.2 us -> 6.02 us
    pallas_call x1, Pallas kernels: 5.08 us -> 7.98 us  [query_call(): pl.pallas_call(functools.partial(query_kernel, query_scale), grid=(rows /...]
    pallas_call x1, Pallas kernels: 44.4 us -> 42.7 us  [attend_call(): pl.pallas_call(functools.partial(attend_kernel, head_dim, len(images)), g...]
  transfers between devices with their start and end apart: 35 -> 35, of which waited for: 17 -> 19; matrix products, arithmetic and copies ran while one was open for 4% -> 4% of each run, Pallas kernels for 6% -> 8%
where the time goes in v1:
time: 155 us
  Pallas kernels  85.6 us (55%)
  starting transfers between devices  34.2 us (22%)
  waiting for transfers between devices  22.6 us (15%)
  local copies, waits for them, and re-layouts  6.03 us (4%)
  other arithmetic  5.72 us (4%)
    pallas_call x1, Pallas kernels, attend_call(): pl.pallas_call(functools.partial(attend_kernel, head_dim, len(images)), g...  42.7 us
    ppermute x35, starting transfers between devices, swap(): return lax.ppermute(array, axis, pairs)  34.2 us
    pallas_call x1, Pallas kernels, render_call(): pl.pallas_call(functools.partial(render_kernel, grid_side, row_span, shar...  25.1 us
    ppermute x35, waiting for transfers between devices, swap(): return lax.ppermute(array, axis, pairs)  22.6 us
    pallas_call x1, Pallas kernels, query_call(): pl.pallas_call(functools.partial(query_kernel, query_scale), grid=(rows /...  7.98 us
    unnamed x69, local copies, waits for them, and re-layouts  6.02 us
    convert_element_type x4, other arithmetic, body(): (kept[j].astype(F32) + swap(passed[j], 'seq', 1).astype(F32)).astype(BF16)  4.76 us
    pallas_call x1, Pallas kernels, weight_grad_call(): pl.pallas_call(functools.partial(weight_grad_kernel, len(parts)), grid=(r...  3.55 us
  transfers between devices with their start and end apart: 35, of which 19 were waited for; matrix products, arithmetic and copies ran while one was open for 4% of the time, Pallas kernels for 8%

profile of v1, /device:TPU:1, one launch (start us, length us, event | category | flops | bytes accessed | tf_op | source)
XLA Modules:
  0.0 155.1 jit_solution(17523585056989701071)
XLA Ops:
  0.6 2.1 %collective-permute-start.1 = (bf16[128,768]{1,0:T(8,128)(2,1)}, bf16[128,768]{1,0:T(8,128)(2,1)S(1)}, u32[]{:S(2)}, u32[]{:S(2)}) collective-permute-start(bf16[128,768]{1,0:T(8,128)(2,1)} %bitcast.44), channel_id=1, source_target_pairs={{0,2},{1,3},{2,0},{3,1},{4,6},{5,7},{6,4},{7,5},{8,10},{9,11},{10,... | collective-permute-start | bytes 589832 | tf_op jit(solution)/shard_map/ppermute | solution.py:50
  2.7 1.2 collective-permute-start.2
  4.0 1.2 collective-permute-start
  5.2 8.0 %queries.1.refs_11_ = bf16[1536,1024]{1,0:T(8,128)(2,1)} custom-call(bf16[1536,1024]{1,0:T(8,128)(2,1)} %bitcast.42, bf16[1024,1024]{1,0:T(8,128)(2,1)} %w_query_ref.1), custom_call_target="tpu_custom_call" | custom-call | flops 3221225472 | bytes 6291456 | tf_op jit(solution)/shard_map/queries/pallas_call | solution.py:86
  13.3 1.3 collective-permute-start.4
  17.0 42.7 %attention_planes.1 = (bf16[1536,1024]{1,0:T(8,128)(2,1)}, bf16[80,1536]{1,0:T(8,128)(2,1)}) custom-call(bf16[128,768]{1,0:T(8,128)(2,1)} %bitcast.48, bf16[128,768]{1,0:T(8,128)(2,1)} %copy-done.29, bf16[128,768]{1,0:T(8,128)(2,1)} %copy-done.26, bf16[128,768]{1,0:T(8,128)(2,1)} %copy-done.30, bf16[128,768]{1,0:T(8,128)(2,1)} %copy-done.27, ...), custom_call_target="tpu_custom_call" | custom-call | flops 9663676416 | bytes 3145728 | tf_op jit(solution)/shard_map/attention_planes/pallas_call | solution.py:168
  59.6 1.7 %collective-permute-start.10 = (bf16[80,1536]{1,0:T(8,128)(2,1)}, bf16[80,1536]{1,0:T(8,128)(2,1)S(1)}, u32[]{:S(2)}, u32[]{:S(2)}) collective-permute-start(bf16[80,1536]{1,0:T(8,128)(2,1)} %get-tuple-element.36.refs_0_), channel_id=1, source_target_pairs={{0,6},{1,7},{2,4},{3,5},{4,2},{5,3},{6,0},{7,1},{8,14},{9,15},{10,... | collective-permute-start | bytes 737288 | tf_op jit(solution)/shard_map/ppermute | solution.py:50
  62.5 1.7 %corners.1 = (f32[3,8,4096]{2,1,0:T(8,128)S(1)}, f32[3,32]{1,0:T(4,128)S(1)}) custom-call(s32[12,4096]{1,0:T(8,128)S(1)} %bitcast.31, bf16[12,4096]{1,0:T(8,128)(2,1)S(1)} %bitcast.34, f32[3,32]{1,0:T(4,128)S(1)} %bitcast.35), custom_call_target="tpu_custom_call" | custom-call | flops 4096000 | bytes 409600 | tf_op jit(solution)/shard_map/corners/pallas_call | solution.py:222
  66.6 1.5 collective-permute-done.10.refs_6_
  68.1 5.3 %collective-permute-done.8.refs_2_ = bf16[80,1536]{1,0:T(8,128)(2,1)S(1)} collective-permute-done((bf16[80,1536]{1,0:T(8,128)(2,1)}, bf16[80,1536]{1,0:T(8,128)(2,1)S(1)}, u32[]{:S(2)}, u32[]{:S(2)}) %collective-permute-start.8) | collective-permute-done | bytes 245792 | tf_op jit(solution)/shard_map/ppermute | solution.py:50
  77.2 25.1 %render.1 = (f32[3,32]{1,0:T(4,128)}, bf16[80,1536]{1,0:T(8,128)(2,1)}, bf16[80,1536]{1,0:T(8,128)(2,1)}, bf16[80,1536]{1,0:T(8,128)(2,1)}, bf16[80,1536]{1,0:T(...) custom-call(bf16[80,1536]{1,0:T(8,128)(2,1)} %get-tuple-element.36.r, ...), custom_call_target="tpu_custom_call" | custom-call | tf_op jit(solution)/shard_map/render/pallas_call | solution.py:435
  110.0 1.7 %add_convert_fusion.refs_3_ = bf16[80,1536]{1,0:T(8,128)(2,1)} fusion(bf16[80,1536]{1,0:T(8,128)(2,1)S(1)} %collective-permute-done.20, bf16[80,1536]{1,0:T(8,128)(2,1)} %get-tuple-element.51), kind=kLoop, calls=%fused_computation | loop fusion | flops 491520 | bytes 737280 | tf_op jit(solution)/shard_map/convert_element_type | solution.py:609
  112.3 5.5 %collective-permute-done.17.refs_1_ = bf16[80,1536]{1,0:T(8,128)(2,1)S(1)} collective-permute-done((bf16[80,1536]{1,0:T(8,128)(2,1)S(1)}, bf16[80,1536]{1,0:T(8,128)(2,1)S(1)}, u32[]{:S(2)}, u32[]{:S(2)}) %collective-permute-start.17) | collective-permute-done | bytes 245792 | tf_op jit(solution)/shard_map/ppermute | solution.py:50
  119.1 3.6 %weight_grad.1 = (f32[4,80,128]{2,1,0:T(8,128)}, f32[4,80,128]{2,1,0:T(8,128)}, bf16[80,1536]{1,0:T(8,128)(2,1)}) custom-call(bf16[80,1536]{1,0:T(8,128)(2,1)} %copy-done.7, bf16[80,1536]{1,0:T(8,128)(2,1)} %copy-done.6, bf16[80,1536]{1,0:T(8,128)(2,1)} %copy-done.5, bf16[80,1536]{1,0:T(8,128)(2,1)} %add_convert_fusion.refs_3_, ...), custom_call_target="tpu_custom_call" | custom-call | tf_op jit(solution)/shard_map/weight_grad/pallas_call | solution.py:491
  122.7 2.3 %collective-permute-start.21 = (f32[4,80,128]{2,1,0:T(8,128)}, f32[4,80,128]{2,1,0:T(8,128)S(1)}, u32[]{:S(2)}, u32[]{:S(2)}) collective-permute-start(f32[4,80,128]{2,1,0:T(8,128)} %get-tuple-element.55), channel_id=1, source_target_pairs={{0,1},{1,0},{2,3},{3,2},{4,5},{5,4},{6,7},{7,6},{8,9},{9,8},{10,11... | collective-permute-start | bytes 491528 | tf_op jit(solution)/shard_map/ppermute | solution.py:50
  124.9 1.2 collective-permute-done.21
  131.1 1.7 %collective-permute-done.24 = f32[80,128]{1,0:T(8,128)S(1)} collective-permute-done((f32[80,128]{1,0:T(8,128)S(1)}, f32[80,128]{1,0:T(8,128)S(1)}, u32[]{:S(2)}, u32[]{:S(2)}) %collective-permute-start.24) | collective-permute-done | bytes 40992 | tf_op jit(solution)/shard_map/ppermute | solution.py:50
  132.8 1.4 collective-permute-start.25
  134.1 2.3 %collective-permute-start.26 = (f32[80,128]{1,0:T(8,128)S(1)}, f32[80,128]{1,0:T(8,128)S(1)}, u32[]{:S(2)}, u32[]{:S(2)}) collective-permute-start(f32[80,128]{1,0:T(8,128)S(1)} %fusion.2), channel_id=1, source_target_pairs={{0,16},{8,24},{16,0},{24,8},{1,17},{9,25},{17,1},{25,9},{2,18},{10... | collective-permute-start | bytes 122888 | tf_op jit(solution)/shard_map/ppermute | solution.py:50
  137.4 2.9 %token_grad.1 = bf16[1536,1024]{1,0:T(8,128)(2,1)} custom-call(bf16[80,1536]{1,0:T(8,128)(2,1)S(1)} %copy-done.1, bf16[80,1024]{1,0:T(8,128)(2,1)S(1)} %bitcast.33), custom_call_target="tpu_custom_call" | custom-call | flops 251658240 | bytes 3145728 | tf_op jit(solution)/shard_map/token_grad/pallas_call | solution.py:521
  142.4 1.5 collective-permute-start.33
  144.0 4.5 %collective-permute-start.28 = (f32[80,128]{1,0:T(8,128)S(1)}, f32[80,128]{1,0:T(8,128)S(1)}, u32[]{:S(2)}, u32[]{:S(2)}) collective-permute-start(f32[80,128]{1,0:T(8,128)S(1)} %add_add_fusion.refs_0_), channel_id=1, source_target_pairs={{0,1},{1,0},{2,3},{3,2},{4,5},{5,4},{6,7},{7,6},{8,9},{9,8},{10,11... | collective-permute-start | bytes 122888 | tf_op jit(solution)/shard_map/ppermute | solution.py:50
  150.0 1.5 collective-permute-start.34
  153.4 1.7 %join_weight_grad.1 = f32[80,1024]{1,0:T(8,128)} custom-call(f32[80,128]{1,0:T(8,128)} %copy-done.16, f32[80,128]{1,0:T(8,128)} %copy-done.20, f32[80,128]{1,0:T(8,128)} %copy-done.17, f32[80,128]{1,0:T(8,128)} %copy-done.21, f32[80,128]{1,0:T(8,128)} %copy-done.18, f32[80,128]{1,0:T(8,128)} %copy-done.22, f32[80,128]{1,0:T(8,128)} %copy-done.19, ...), custom_call_target="tpu_custom_call" | custom-call | tf_op jit(solution)/shard_map/join_weight_grad/pallas_call | solution.py:548
  (130 shorter events, 30.5 us)
Async XLA Ops:
  0.6 12.6 %collective-permute-start.1 = (bf16[128,768]{1,0:T(8,128)(2,1)}, bf16[128,768]{1,0:T(8,128)(2,1)S(1)}, u32[]{:S(2)}, u32[]{:S(2)}) collective-permute-start(bf16[128,768]{1,0:T(8,128)(2,1)} %bitcast.44), channel_id=1, source_target_pairs={{0,2},{1,3},{2,0},{3,1},{4,6},{5,7},{6,4},{7,5},{8,10},{9,11},{10,... | collective-permute-start | bytes 589832 | tf_op jit(solution)/shard_map/ppermute | solution.py:50
  2.7 10.5 %collective-permute-start.2 = (bf16[128,768]{1,0:T(8,128)(2,1)}, bf16[128,768]{1,0:T(8,128)(2,1)S(1)}, u32[]{:S(2)}, u32[]{:S(2)}) collective-permute-start(bf16[128,768]{1,0:T(8,128)(2,1)} %bitcast.45), channel_id=1, source_target_pairs={{0,4},{1,5},{2,6},{3,7},{4,0},{5,1},{6,2},{7,3},{8,12},{9,13},{10,... | collective-permute-start | bytes 589832 | tf_op jit(solution)/shard_map/ppermute | solution.py:50
  4.0 9.3 %collective-permute-start.3 = (bf16[128,768]{1,0:T(8,128)(2,1)}, bf16[128,768]{1,0:T(8,128)(2,1)S(1)}, u32[]{:S(2)}, u32[]{:S(2)}) collective-permute-start(bf16[128,768]{1,0:T(8,128)(2,1)} %bitcast.46), channel_id=1, source_target_pairs={{0,6},{1,7},{2,4},{3,5},{4,2},{5,3},{6,0},{7,1},{8,14},{9,15},{10,... | collective-permute-start | bytes 589832 | tf_op jit(solution)/shard_map/ppermute | solution.py:50
  4.0 11.1 %collective-permute-start = (bf16[128,768]{1,0:T(8,128)(2,1)}, bf16[128,768]{1,0:T(8,128)(2,1)S(1)}, u32[]{:S(2)}, u32[]{:S(2)}) collective-permute-start(bf16[128,768]{1,0:T(8,128)(2,1)} %bitcast.47), channel_id=1, source_target_pairs={{0,1},{1,0},{2,3},{3,2},{4,5},{5,4},{6,7},{7,6},{8,9},{9,8},{10,11... | collective-permute-start | bytes 589832 | tf_op jit(solution)/shard_map/ppermute | solution.py:50
  59.6 8.5 %collective-permute-start.10 = (bf16[80,1536]{1,0:T(8,128)(2,1)}, bf16[80,1536]{1,0:T(8,128)(2,1)S(1)}, u32[]{:S(2)}, u32[]{:S(2)}) collective-permute-start(bf16[80,1536]{1,0:T(8,128)(2,1)} %get-tuple-element.36.refs_0_), channel_id=1, source_target_pairs={{0,6},{1,7},{2,4},{3,5},{4,2},{5,3},{6,0},{7,1},{8,14},{9,15},{10,... | collective-permute-start | bytes 737288 | tf_op jit(solution)/shard_map/ppermute | solution.py:50
  61.4 12.1 %collective-permute-start.8 = (bf16[80,1536]{1,0:T(8,128)(2,1)}, bf16[80,1536]{1,0:T(8,128)(2,1)S(1)}, u32[]{:S(2)}, u32[]{:S(2)}) collective-permute-start(bf16[80,1536]{1,0:T(8,128)(2,1)} %get-tuple-element.36.refs_0_), channel_id=1, source_target_pairs={{0,2},{1,3},{2,0},{3,1},{4,6},{5,7},{6,4},{7,5},{8,10},{9,11},{10,... | collective-permute-start | bytes 737288 | tf_op jit(solution)/shard_map/ppermute | solution.py:50
  62.1 11.8 %collective-permute-start.9 = (bf16[80,1536]{1,0:T(8,128)(2,1)}, bf16[80,1536]{1,0:T(8,128)(2,1)S(1)}, u32[]{:S(2)}, u32[]{:S(2)}) collective-permute-start(bf16[80,1536]{1,0:T(8,128)(2,1)} %get-tuple-element.36.refs_0_), channel_id=1, source_target_pairs={{0,4},{1,5},{2,6},{3,7},{4,0},{5,1},{6,2},{7,3},{8,12},{9,13},{10,... | collective-permute-start | bytes 737288 | tf_op jit(solution)/shard_map/ppermute | solution.py:50
  65.5 9.6 %collective-permute-start.7 = (bf16[80,1536]{1,0:T(8,128)(2,1)}, bf16[80,1536]{1,0:T(8,128)(2,1)S(1)}, u32[]{:S(2)}, u32[]{:S(2)}) collective-permute-start(bf16[80,1536]{1,0:T(8,128)(2,1)} %get-tuple-element.36.refs_0_), channel_id=1, source_target_pairs={{0,1},{1,0},{2,3},{3,2},{4,5},{5,4},{6,7},{7,6},{8,9},{9,8},{10,11... | collective-permute-start | bytes 737288 | tf_op jit(solution)/shard_map/ppermute | solution.py:50
  102.7 7.3 %collective-permute-start.20 = (bf16[80,1536]{1,0:T(8,128)(2,1)}, bf16[80,1536]{1,0:T(8,128)(2,1)S(1)}, u32[]{:S(2)}, u32[]{:S(2)}) collective-permute-start(bf16[80,1536]{1,0:T(8,128)(2,1)} %get-tuple-element.52), channel_id=1, source_target_pairs={{0,1},{1,0},{2,3},{3,2},{4,5},{5,4},{6,7},{7,6},{8,9},{9,8},{10,11... | collective-permute-start | bytes 737288 | tf_op jit(solution)/shard_map/ppermute | solution.py:50
  103.2 4.8 %collective-permute-start.14 = (bf16[80,1536]{1,0:T(8,128)(2,1)}, bf16[80,1536]{1,0:T(8,128)(2,1)S(1)}, u32[]{:S(2)}, u32[]{:S(2)}) collective-permute-start(bf16[80,1536]{1,0:T(8,128)(2,1)} %get-tuple-element.46), channel_id=1, source_target_pairs={{0,1},{1,0},{2,3},{3,2},{4,5},{5,4},{6,7},{7,6},{8,9},{9,8},{10,11... | collective-permute-start | bytes 737288 | tf_op jit(solution)/shard_map/ppermute | solution.py:50
  105.1 7.3 %collective-permute-start.19 = (bf16[80,1536]{1,0:T(8,128)(2,1)S(1)}, bf16[80,1536]{1,0:T(8,128)(2,1)S(1)}, u32[]{:S(2)}, u32[]{:S(2)}) collective-permute-start(bf16[80,1536]{1,0:T(8,128)(2,1)S(1)} %add_convert_fusion.1), channel_id=1, source_target_pairs={{0,2},{1,3},{2,0},{3,1},{4,6},{5,7},{6,4},{7,5},{8,10},{9,11},{10,... | collective-permute-start | bytes 737288 | tf_op jit(solution)/shard_map/ppermute | solution.py:50
  106.9 10.9 %collective-permute-start.17 = (bf16[80,1536]{1,0:T(8,128)(2,1)S(1)}, bf16[80,1536]{1,0:T(8,128)(2,1)S(1)}, u32[]{:S(2)}, u32[]{:S(2)}) collective-permute-start(bf16[80,1536]{1,0:T(8,128)(2,1)S(1)} %add_convert_fusion.2), channel_id=1, source_target_pairs={{0,4},{1,5},{2,6},{3,7},{4,0},{5,1},{6,2},{7,3},{8,12},{9,13},{10,... | collective-permute-start | bytes 737288 | tf_op jit(solution)/shard_map/ppermute | solution.py:50
  109.1 9.4 %collective-permute-start.15 = (bf16[80,1536]{1,0:T(8,128)(2,1)S(1)}, bf16[80,1536]{1,0:T(8,128)(2,1)S(1)}, u32[]{:S(2)}, u32[]{:S(2)}) collective-permute-start(bf16[80,1536]{1,0:T(8,128)(2,1)S(1)} %add_convert_fusion.3), channel_id=1, source_target_pairs={{0,6},{1,7},{2,4},{3,5},{4,2},{5,3},{6,0},{7,1},{8,14},{9,15},{10,... | collective-permute-start | bytes 737288 | tf_op jit(solution)/shard_map/ppermute | solution.py:50
  122.7 3.5 %collective-permute-start.21 = (f32[4,80,128]{2,1,0:T(8,128)}, f32[4,80,128]{2,1,0:T(8,128)S(1)}, u32[]{:S(2)}, u32[]{:S(2)}) collective-permute-start(f32[4,80,128]{2,1,0:T(8,128)} %get-tuple-element.55), channel_id=1, source_target_pairs={{0,1},{1,0},{2,3},{3,2},{4,5},{5,4},{6,7},{7,6},{8,9},{9,8},{10,11... | collective-permute-start | bytes 491528 | tf_op jit(solution)/shard_map/ppermute | solution.py:50
  127.9 3.1 %collective-permute-start.23 = (f32[80,128]{1,0:T(8,128)S(1)}, f32[80,128]{1,0:T(8,128)S(1)}, u32[]{:S(2)}, u32[]{:S(2)}) collective-permute-start(f32[80,128]{1,0:T(8,128)S(1)} %get-tuple-element.66), channel_id=1, source_target_pairs={{0,4},{1,5},{2,6},{3,7},{4,0},{5,1},{6,2},{7,3},{8,12},{9,13},{10,... | collective-permute-start | bytes 122888 | tf_op jit(solution)/shard_map/ppermute | solution.py:50
  129.0 3.8 %collective-permute-start.24 = (f32[80,128]{1,0:T(8,128)S(1)}, f32[80,128]{1,0:T(8,128)S(1)}, u32[]{:S(2)}, u32[]{:S(2)}) collective-permute-start(f32[80,128]{1,0:T(8,128)S(1)} %get-tuple-element.65), channel_id=1, source_target_pairs={{0,6},{1,7},{2,4},{3,5},{4,2},{5,3},{6,0},{7,1},{8,14},{9,15},{10,... | collective-permute-start | bytes 122888 | tf_op jit(solution)/shard_map/ppermute | solution.py:50
  132.8 7.6 %collective-permute-start.25 = (f32[80,128]{1,0:T(8,128)S(1)}, f32[80,128]{1,0:T(8,128)S(1)}, u32[]{:S(2)}, u32[]{:S(2)}) collective-permute-start(f32[80,128]{1,0:T(8,128)S(1)} %fusion.2), channel_id=1, source_target_pairs={{0,8},{8,0},{16,24},{24,16},{1,9},{9,1},{17,25},{25,17},{2,10},{10... | collective-permute-start | bytes 122888 | tf_op jit(solution)/shard_map/ppermute | solution.py:50
  134.1 6.2 %collective-permute-start.26 = (f32[80,128]{1,0:T(8,128)S(1)}, f32[80,128]{1,0:T(8,128)S(1)}, u32[]{:S(2)}, u32[]{:S(2)}) collective-permute-start(f32[80,128]{1,0:T(8,128)S(1)} %fusion.2), channel_id=1, source_target_pairs={{0,16},{8,24},{16,0},{24,8},{1,17},{9,25},{17,1},{25,9},{2,18},{10... | collective-permute-start | bytes 122888 | tf_op jit(solution)/shard_map/ppermute | solution.py:50
  136.5 4.8 %collective-permute-start.27 = (f32[80,128]{1,0:T(8,128)S(1)}, f32[80,128]{1,0:T(8,128)S(1)}, u32[]{:S(2)}, u32[]{:S(2)}) collective-permute-start(f32[80,128]{1,0:T(8,128)S(1)} %fusion.2), channel_id=1, source_target_pairs={{0,24},{8,16},{16,8},{24,0},{1,25},{9,17},{17,9},{25,1},{2,26},{10... | collective-permute-start | bytes 122888 | tf_op jit(solution)/shard_map/ppermute | solution.py:50
  141.3 7.2 %collective-permute-start.29 = (f32[80,128]{1,0:T(8,128)S(1)}, f32[80,128]{1,0:T(8,128)S(1)}, u32[]{:S(2)}, u32[]{:S(2)}) collective-permute-start(f32[80,128]{1,0:T(8,128)S(1)} %add_add_fusion.refs_0_), channel_id=1, source_target_pairs={{0,2},{1,3},{2,0},{3,1},{4,6},{5,7},{6,4},{7,5},{8,10},{9,11},{10,... | collective-permute-start | bytes 122888 | tf_op jit(solution)/shard_map/ppermute | solution.py:50
  142.1 6.9 %collective-permute-start.31 = (f32[80,128]{1,0:T(8,128)S(1)}, f32[80,128]{1,0:T(8,128)S(1)}, u32[]{:S(2)}, u32[]{:S(2)}) collective-permute-start(f32[80,128]{1,0:T(8,128)S(1)} %add_add_fusion.refs_0_), channel_id=1, source_target_pairs={{0,4},{1,5},{2,6},{3,7},{4,0},{5,1},{6,2},{7,3},{8,12},{9,13},{10,... | collective-permute-start | bytes 122888 | tf_op jit(solution)/shard_map/ppermute | solution.py:50
  142.4 7.6 %collective-permute-start.33 = (f32[80,128]{1,0:T(8,128)S(1)}, f32[80,128]{1,0:T(8,128)S(1)}, u32[]{:S(2)}, u32[]{:S(2)}) collective-permute-start(f32[80,128]{1,0:T(8,128)S(1)} %add_add_fusion.refs_0_), channel_id=1, source_target_pairs={{0,6},{1,7},{2,4},{3,5},{4,2},{5,3},{6,0},{7,1},{8,14},{9,15},{10,... | collective-permute-start | bytes 122888 | tf_op jit(solution)/shard_map/ppermute | solution.py:50
  144.0 8.1 %collective-permute-start.28 = (f32[80,128]{1,0:T(8,128)S(1)}, f32[80,128]{1,0:T(8,128)S(1)}, u32[]{:S(2)}, u32[]{:S(2)}) collective-permute-start(f32[80,128]{1,0:T(8,128)S(1)} %add_add_fusion.refs_0_), channel_id=1, source_target_pairs={{0,1},{1,0},{2,3},{3,2},{4,5},{5,4},{6,7},{7,6},{8,9},{9,8},{10,11... | collective-permute-start | bytes 122888 | tf_op jit(solution)/shard_map/ppermute | solution.py:50
  148.5 3.6 %collective-permute-start.30 = (f32[80,128]{1,0:T(8,128)S(1)}, f32[80,128]{1,0:T(8,128)S(1)}, u32[]{:S(2)}, u32[]{:S(2)}) collective-permute-start(f32[80,128]{1,0:T(8,128)S(1)} %collective-permute-done.29.refs_2_), channel_id=1, source_target_pairs={{0,1},{1,0},{2,3},{3,2},{4,5},{5,4},{6,7},{7,6},{8,9},{9,8},{10,11... | collective-permute-start | bytes 122888 | tf_op jit(solution)/shard_map/ppermute | solution.py:50
  (44 other events, 280.7 us)

commit v2 on v1

--- a/solution.py
+++ b/solution.py
@@ -51,7 +51,8 @@
 
 
 def from_chips(piece):
-    return [swap(piece, "seq", k) for k in range(2, lax.axis_size("seq"), 2)]
+    far = {k: swap(piece, "seq", k) for k in reversed(range(2, lax.axis_size("seq"), 2))}
+    return [far[k] for k in sorted(far)]
 
 
 def with_other_core(pieces):
@@ -611,9 +612,9 @@
     kept, passed, grad = weight_grad_call(parts, plane_in, shares)
     pairs = kept + swap(passed, "seq", 1)
     chunk = pairs[0]
-    for j in range(1, shares // 2):
+    for j in reversed(range(1, shares // 2)):
         chunk = chunk + swap(pairs[j], "seq", 2 * j)
-    others = [swap(chunk, "dp", k) for k in range(1, lax.axis_size("dp"))]
+    others = [swap(chunk, "dp", k) for k in reversed(range(1, lax.axis_size("dp")))]
     token_grad = token_grad_call(grad, w_plane_t)
     others, token_grad = lax.optimization_barrier((others, token_grad))
     scenes = sum(others, chunk)

time: 155 us -> 154 us (level)
  transfers between devices with their start and end apart: 35 -> 35, of which waited for: 19 -> 17; matrix products, arithmetic and copies ran while one was open for 4% -> 4% of each run, Pallas kernels for 8% -> 8%
where the time goes in v2:
time: 154 us
  Pallas kernels  85.6 us (56%)
  starting transfers between devices  34.2 us (22%)
  waiting for transfers between devices  21.1 us (14%)
  local copies, waits for them, and re-layouts  6.03 us (4%)
  other arithmetic  5.73 us (4%)
    pallas_call x1, Pallas kernels, attend_call(): pl.pallas_call(functools.partial(attend_kernel, head_dim, len(images)), g...  42.7 us
    ppermute x35, starting transfers between devices, swap(): return lax.ppermute(array, axis, pairs)  34.2 us
    pallas_call x1, Pallas kernels, render_call(): pl.pallas_call(functools.partial(render_kernel, grid_side, row_span, shar...  25.1 us
    ppermute x35, waiting for transfers between devices, swap(): return lax.ppermute(array, axis, pairs)  21.1 us
    pallas_call x1, Pallas kernels, query_call(): pl.pallas_call(functools.partial(query_kernel, query_scale), grid=(rows /...  7.98 us
    unnamed x69, local copies, waits for them, and re-layouts  6.02 us
    convert_element_type x4, other arithmetic, body(): (kept[j].astype(F32) + swap(passed[j], 'seq', 1).astype(F32)).astype(BF16)  4.76 us
    pallas_call x1, Pallas kernels, weight_grad_call(): pl.pallas_call(functools.partial(weight_grad_kernel, len(parts)), grid=(r...  3.55 us
  transfers between devices with their start and end apart: 35, of which 17 were waited for; matrix products, arithmetic and copies ran while one was open for 4% of the time, Pallas kernels for 8%

profile of v2, /device:TPU:1, one launch (start us, length us, event | category | flops | bytes accessed | tf_op | source)
XLA Modules:
  0.0 153.5 jit_solution(15240304283215847358)
XLA Ops:
  0.6 2.1 %collective-permute-start.1 = (bf16[128,768]{1,0:T(8,128)(2,1)}, bf16[128,768]{1,0:T(8,128)(2,1)S(1)}, u32[]{:S(2)}, u32[]{:S(2)}) collective-permute-start(bf16[128,768]{1,0:T(8,128)(2,1)} %bitcast.44), channel_id=1, source_target_pairs={{0,2},{1,3},{2,0},{3,1},{4,6},{5,7},{6,4},{7,5},{8,10},{9,11},{10,... | collective-permute-start | bytes 589832 | tf_op jit(solution)/shard_map/ppermute | solution.py:50
  2.7 1.2 collective-permute-start.2
  4.0 1.2 collective-permute-start
  5.2 8.0 %queries.1.refs_11_ = bf16[1536,1024]{1,0:T(8,128)(2,1)} custom-call(bf16[1536,1024]{1,0:T(8,128)(2,1)} %bitcast.42, bf16[1024,1024]{1,0:T(8,128)(2,1)} %w_query_ref.1), custom_call_target="tpu_custom_call" | custom-call | flops 3221225472 | bytes 6291456 | tf_op jit(solution)/shard_map/queries/pallas_call | solution.py:87
  13.3 1.3 collective-permute-start.4
  17.0 42.7 %attention_planes.1 = (bf16[1536,1024]{1,0:T(8,128)(2,1)}, bf16[80,1536]{1,0:T(8,128)(2,1)}) custom-call(bf16[128,768]{1,0:T(8,128)(2,1)} %bitcast.48, bf16[128,768]{1,0:T(8,128)(2,1)} %copy-done.29, bf16[128,768]{1,0:T(8,128)(2,1)} %copy-done.26, bf16[128,768]{1,0:T(8,128)(2,1)} %copy-done.30, bf16[128,768]{1,0:T(8,128)(2,1)} %copy-done.27, ...), custom_call_target="tpu_custom_call" | custom-call | flops 9663676416 | bytes 3145728 | tf_op jit(solution)/shard_map/attention_planes/pallas_call | solution.py:169
  59.6 1.7 %collective-permute-start.10 = (bf16[80,1536]{1,0:T(8,128)(2,1)}, bf16[80,1536]{1,0:T(8,128)(2,1)S(1)}, u32[]{:S(2)}, u32[]{:S(2)}) collective-permute-start(bf16[80,1536]{1,0:T(8,128)(2,1)} %get-tuple-element.36.refs_0_), channel_id=1, source_target_pairs={{0,6},{1,7},{2,4},{3,5},{4,2},{5,3},{6,0},{7,1},{8,14},{9,15},{10,... | collective-permute-start | bytes 737288 | tf_op jit(solution)/shard_map/ppermute | solution.py:50
  62.5 1.7 %corners.1 = (f32[3,8,4096]{2,1,0:T(8,128)S(1)}, f32[3,32]{1,0:T(4,128)S(1)}) custom-call(s32[12,4096]{1,0:T(8,128)S(1)} %bitcast.31, bf16[12,4096]{1,0:T(8,128)(2,1)S(1)} %bitcast.34, f32[3,32]{1,0:T(4,128)S(1)} %bitcast.35), custom_call_target="tpu_custom_call" | custom-call | flops 4096000 | bytes 409600 | tf_op jit(solution)/shard_map/corners/pallas_call | solution.py:223
  66.6 1.5 collective-permute-done.10.refs_6_
  68.1 5.3 %collective-permute-done.8.refs_2_ = bf16[80,1536]{1,0:T(8,128)(2,1)S(1)} collective-permute-done((bf16[80,1536]{1,0:T(8,128)(2,1)}, bf16[80,1536]{1,0:T(8,128)(2,1)S(1)}, u32[]{:S(2)}, u32[]{:S(2)}) %collective-permute-start.8) | collective-permute-done | bytes 245792 | tf_op jit(solution)/shard_map/ppermute | solution.py:50
  77.2 25.1 %render.1 = (f32[3,32]{1,0:T(4,128)}, bf16[80,1536]{1,0:T(8,128)(2,1)}, bf16[80,1536]{1,0:T(8,128)(2,1)}, bf16[80,1536]{1,0:T(8,128)(2,1)}, bf16[80,1536]{1,0:T(...) custom-call(bf16[80,1536]{1,0:T(8,128)(2,1)} %get-tuple-element.36.r, ...), custom_call_target="tpu_custom_call" | custom-call | tf_op jit(solution)/shard_map/render/pallas_call | solution.py:436
  106.9 1.1 collective-permute-start.17
  110.0 1.7 %add_convert_fusion.refs_3_ = bf16[80,1536]{1,0:T(8,128)(2,1)} fusion(bf16[80,1536]{1,0:T(8,128)(2,1)S(1)} %collective-permute-done.20, bf16[80,1536]{1,0:T(8,128)(2,1)} %get-tuple-element.51), kind=kLoop, calls=%fused_computation | loop fusion | flops 491520 | bytes 737280 | tf_op jit(solution)/shard_map/convert_element_type | solution.py:610
  112.3 5.5 %collective-permute-done.17.refs_1_ = bf16[80,1536]{1,0:T(8,128)(2,1)S(1)} collective-permute-done((bf16[80,1536]{1,0:T(8,128)(2,1)S(1)}, bf16[80,1536]{1,0:T(8,128)(2,1)S(1)}, u32[]{:S(2)}, u32[]{:S(2)}) %collective-permute-start.17) | collective-permute-done | bytes 245792 | tf_op jit(solution)/shard_map/ppermute | solution.py:50
  119.1 3.6 %weight_grad.1 = (f32[4,80,128]{2,1,0:T(8,128)}, f32[4,80,128]{2,1,0:T(8,128)}, bf16[80,1536]{1,0:T(8,128)(2,1)}) custom-call(bf16[80,1536]{1,0:T(8,128)(2,1)} %copy-done.7, bf16[80,1536]{1,0:T(8,128)(2,1)} %copy-done.6, bf16[80,1536]{1,0:T(8,128)(2,1)} %copy-done.5, bf16[80,1536]{1,0:T(8,128)(2,1)} %add_convert_fusion.refs_3_, ...), custom_call_target="tpu_custom_call" | custom-call | tf_op jit(solution)/shard_map/weight_grad/pallas_call | solution.py:492
  122.7 2.3 %collective-permute-start.21 = (f32[4,80,128]{2,1,0:T(8,128)}, f32[4,80,128]{2,1,0:T(8,128)S(1)}, u32[]{:S(2)}, u32[]{:S(2)}) collective-permute-start(f32[4,80,128]{2,1,0:T(8,128)} %get-tuple-element.55), channel_id=1, source_target_pairs={{0,1},{1,0},{2,3},{3,2},{4,5},{5,4},{6,7},{7,6},{8,9},{9,8},{10,11... | collective-permute-start | bytes 491528 | tf_op jit(solution)/shard_map/ppermute | solution.py:50
  124.9 1.2 collective-permute-done.21
  127.1 1.6 %collective-permute-start.22 = (f32[80,128]{1,0:T(8,128)S(1)}, f32[80,128]{1,0:T(8,128)S(1)}, u32[]{:S(2)}, u32[]{:S(2)}) collective-permute-start(f32[80,128]{1,0:T(8,128)S(1)} %get-tuple-element.64), channel_id=1, source_target_pairs={{0,6},{1,7},{2,4},{3,5},{4,2},{5,3},{6,0},{7,1},{8,14},{9,15},{10,... | collective-permute-start | bytes 122888 | tf_op jit(solution)/shard_map/ppermute | solution.py:50
  132.1 3.4 %collective-permute-start.25 = (f32[80,128]{1,0:T(8,128)S(1)}, f32[80,128]{1,0:T(8,128)S(1)}, u32[]{:S(2)}, u32[]{:S(2)}) collective-permute-start(f32[80,128]{1,0:T(8,128)S(1)} %fusion.2), channel_id=1, source_target_pairs={{0,24},{8,16},{16,8},{24,0},{1,25},{9,17},{17,9},{25,1},{2,26},{10... | collective-permute-start | bytes 122888 | tf_op jit(solution)/shard_map/ppermute | solution.py:50
  136.8 2.9 %token_grad.1 = bf16[1536,1024]{1,0:T(8,128)(2,1)} custom-call(bf16[80,1536]{1,0:T(8,128)(2,1)S(1)} %copy-done.1, bf16[80,1024]{1,0:T(8,128)(2,1)S(1)} %bitcast.33), custom_call_target="tpu_custom_call" | custom-call | flops 251658240 | bytes 3145728 | tf_op jit(solution)/shard_map/token_grad/pallas_call | solution.py:522
  140.6 1.2 collective-permute-start.31
  142.5 3.7 %collective-permute-start.28 = (f32[80,128]{1,0:T(8,128)S(1)}, f32[80,128]{1,0:T(8,128)S(1)}, u32[]{:S(2)}, u32[]{:S(2)}) collective-permute-start(f32[80,128]{1,0:T(8,128)S(1)} %add_add_fusion.refs_0_), channel_id=1, source_target_pairs={{0,1},{1,0},{2,3},{3,2},{4,5},{5,4},{6,7},{7,6},{8,9},{9,8},{10,11... | collective-permute-start | bytes 122888 | tf_op jit(solution)/shard_map/ppermute | solution.py:50
  147.7 2.3 %collective-permute-start.34 = (f32[80,128]{1,0:T(8,128)S(1)}, f32[80,128]{1,0:T(8,128)S(1)}, u32[]{:S(2)}, u32[]{:S(2)}) collective-permute-start(f32[80,128]{1,0:T(8,128)S(1)} %collective-permute-done.33.refs_6_), channel_id=1, source_target_pairs={{0,1},{1,0},{2,3},{3,2},{4,5},{5,4},{6,7},{7,6},{8,9},{9,8},{10,11... | collective-permute-start | bytes 122888 | tf_op jit(solution)/shard_map/ppermute | solution.py:50
  151.8 1.7 %join_weight_grad.1 = f32[80,1024]{1,0:T(8,128)} custom-call(f32[80,128]{1,0:T(8,128)} %copy-done.16, f32[80,128]{1,0:T(8,128)} %copy-done.20, f32[80,128]{1,0:T(8,128)} %copy-done.17, f32[80,128]{1,0:T(8,128)} %copy-done.21, f32[80,128]{1,0:T(8,128)} %copy-done.18, f32[80,128]{1,0:T(8,128)} %copy-done.22, f32[80,128]{1,0:T(8,128)} %copy-done.19, ...), custom_call_target="tpu_custom_call" | custom-call | tf_op jit(solution)/shard_map/join_weight_grad/pallas_call | solution.py:549
  (130 shorter events, 28.6 us)
Async XLA Ops:
  0.6 12.6 %collective-permute-start.1 = (bf16[128,768]{1,0:T(8,128)(2,1)}, bf16[128,768]{1,0:T(8,128)(2,1)S(1)}, u32[]{:S(2)}, u32[]{:S(2)}) collective-permute-start(bf16[128,768]{1,0:T(8,128)(2,1)} %bitcast.44), channel_id=1, source_target_pairs={{0,2},{1,3},{2,0},{3,1},{4,6},{5,7},{6,4},{7,5},{8,10},{9,11},{10,... | collective-permute-start | bytes 589832 | tf_op jit(solution)/shard_map/ppermute | solution.py:50
  2.7 10.5 %collective-permute-start.2 = (bf16[128,768]{1,0:T(8,128)(2,1)}, bf16[128,768]{1,0:T(8,128)(2,1)S(1)}, u32[]{:S(2)}, u32[]{:S(2)}) collective-permute-start(bf16[128,768]{1,0:T(8,128)(2,1)} %bitcast.45), channel_id=1, source_target_pairs={{0,4},{1,5},{2,6},{3,7},{4,0},{5,1},{6,2},{7,3},{8,12},{9,13},{10,... | collective-permute-start | bytes 589832 | tf_op jit(solution)/shard_map/ppermute | solution.py:50
  4.0 9.3 %collective-permute-start.3 = (bf16[128,768]{1,0:T(8,128)(2,1)}, bf16[128,768]{1,0:T(8,128)(2,1)S(1)}, u32[]{:S(2)}, u32[]{:S(2)}) collective-permute-start(bf16[128,768]{1,0:T(8,128)(2,1)} %bitcast.46), channel_id=1, source_target_pairs={{0,6},{1,7},{2,4},{3,5},{4,2},{5,3},{6,0},{7,1},{8,14},{9,15},{10,... | collective-permute-start | bytes 589832 | tf_op jit(solution)/shard_map/ppermute | solution.py:50
  4.0 11.1 %collective-permute-start = (bf16[128,768]{1,0:T(8,128)(2,1)}, bf16[128,768]{1,0:T(8,128)(2,1)S(1)}, u32[]{:S(2)}, u32[]{:S(2)}) collective-permute-start(bf16[128,768]{1,0:T(8,128)(2,1)} %bitcast.47), channel_id=1, source_target_pairs={{0,1},{1,0},{2,3},{3,2},{4,5},{5,4},{6,7},{7,6},{8,9},{9,8},{10,11... | collective-permute-start | bytes 589832 | tf_op jit(solution)/shard_map/ppermute | solution.py:50
  59.6 8.5 %collective-permute-start.10 = (bf16[80,1536]{1,0:T(8,128)(2,1)}, bf16[80,1536]{1,0:T(8,128)(2,1)S(1)}, u32[]{:S(2)}, u32[]{:S(2)}) collective-permute-start(bf16[80,1536]{1,0:T(8,128)(2,1)} %get-tuple-element.36.refs_0_), channel_id=1, source_target_pairs={{0,6},{1,7},{2,4},{3,5},{4,2},{5,3},{6,0},{7,1},{8,14},{9,15},{10,... | collective-permute-start | bytes 737288 | tf_op jit(solution)/shard_map/ppermute | solution.py:50
  61.4 12.1 %collective-permute-start.8 = (bf16[80,1536]{1,0:T(8,128)(2,1)}, bf16[80,1536]{1,0:T(8,128)(2,1)S(1)}, u32[]{:S(2)}, u32[]{:S(2)}) collective-permute-start(bf16[80,1536]{1,0:T(8,128)(2,1)} %get-tuple-element.36.refs_0_), channel_id=1, source_target_pairs={{0,2},{1,3},{2,0},{3,1},{4,6},{5,7},{6,4},{7,5},{8,10},{9,11},{10,... | collective-permute-start | bytes 737288 | tf_op jit(solution)/shard_map/ppermute | solution.py:50
  62.1 11.8 %collective-permute-start.9 = (bf16[80,1536]{1,0:T(8,128)(2,1)}, bf16[80,1536]{1,0:T(8,128)(2,1)S(1)}, u32[]{:S(2)}, u32[]{:S(2)}) collective-permute-start(bf16[80,1536]{1,0:T(8,128)(2,1)} %get-tuple-element.36.refs_0_), channel_id=1, source_target_pairs={{0,4},{1,5},{2,6},{3,7},{4,0},{5,1},{6,2},{7,3},{8,12},{9,13},{10,... | collective-permute-start | bytes 737288 | tf_op jit(solution)/shard_map/ppermute | solution.py:50
  65.5 9.6 %collective-permute-start.7 = (bf16[80,1536]{1,0:T(8,128)(2,1)}, bf16[80,1536]{1,0:T(8,128)(2,1)S(1)}, u32[]{:S(2)}, u32[]{:S(2)}) collective-permute-start(bf16[80,1536]{1,0:T(8,128)(2,1)} %get-tuple-element.36.refs_0_), channel_id=1, source_target_pairs={{0,1},{1,0},{2,3},{3,2},{4,5},{5,4},{6,7},{7,6},{8,9},{9,8},{10,11... | collective-permute-start | bytes 737288 | tf_op jit(solution)/shard_map/ppermute | solution.py:50
  102.7 7.3 %collective-permute-start.20 = (bf16[80,1536]{1,0:T(8,128)(2,1)}, bf16[80,1536]{1,0:T(8,128)(2,1)S(1)}, u32[]{:S(2)}, u32[]{:S(2)}) collective-permute-start(bf16[80,1536]{1,0:T(8,128)(2,1)} %get-tuple-element.52), channel_id=1, source_target_pairs={{0,1},{1,0},{2,3},{3,2},{4,5},{5,4},{6,7},{7,6},{8,9},{9,8},{10,11... | collective-permute-start | bytes 737288 | tf_op jit(solution)/shard_map/ppermute | solution.py:50
  103.2 4.8 %collective-permute-start.14 = (bf16[80,1536]{1,0:T(8,128)(2,1)}, bf16[80,1536]{1,0:T(8,128)(2,1)S(1)}, u32[]{:S(2)}, u32[]{:S(2)}) collective-permute-start(bf16[80,1536]{1,0:T(8,128)(2,1)} %get-tuple-element.46), channel_id=1, source_target_pairs={{0,1},{1,0},{2,3},{3,2},{4,5},{5,4},{6,7},{7,6},{8,9},{9,8},{10,11... | collective-permute-start | bytes 737288 | tf_op jit(solution)/shard_map/ppermute | solution.py:50
  105.1 7.3 %collective-permute-start.19 = (bf16[80,1536]{1,0:T(8,128)(2,1)S(1)}, bf16[80,1536]{1,0:T(8,128)(2,1)S(1)}, u32[]{:S(2)}, u32[]{:S(2)}) collective-permute-start(bf16[80,1536]{1,0:T(8,128)(2,1)S(1)} %add_convert_fusion.1), channel_id=1, source_target_pairs={{0,2},{1,3},{2,0},{3,1},{4,6},{5,7},{6,4},{7,5},{8,10},{9,11},{10,... | collective-permute-start | bytes 737288 | tf_op jit(solution)/shard_map/ppermute | solution.py:50
  106.9 10.9 %collective-permute-start.17 = (bf16[80,1536]{1,0:T(8,128)(2,1)S(1)}, bf16[80,1536]{1,0:T(8,128)(2,1)S(1)}, u32[]{:S(2)}, u32[]{:S(2)}) collective-permute-start(bf16[80,1536]{1,0:T(8,128)(2,1)S(1)} %add_convert_fusion.2), channel_id=1, source_target_pairs={{0,4},{1,5},{2,6},{3,7},{4,0},{5,1},{6,2},{7,3},{8,12},{9,13},{10,... | collective-permute-start | bytes 737288 | tf_op jit(solution)/shard_map/ppermute | solution.py:50
  109.1 9.4 %collective-permute-start.15 = (bf16[80,1536]{1,0:T(8,128)(2,1)S(1)}, bf16[80,1536]{1,0:T(8,128)(2,1)S(1)}, u32[]{:S(2)}, u32[]{:S(2)}) collective-permute-start(bf16[80,1536]{1,0:T(8,128)(2,1)S(1)} %add_convert_fusion.3), channel_id=1, source_target_pairs={{0,6},{1,7},{2,4},{3,5},{4,2},{5,3},{6,0},{7,1},{8,14},{9,15},{10,... | collective-permute-start | bytes 737288 | tf_op jit(solution)/shard_map/ppermute | solution.py:50
  122.7 3.5 %collective-permute-start.21 = (f32[4,80,128]{2,1,0:T(8,128)}, f32[4,80,128]{2,1,0:T(8,128)S(1)}, u32[]{:S(2)}, u32[]{:S(2)}) collective-permute-start(f32[4,80,128]{2,1,0:T(8,128)} %get-tuple-element.55), channel_id=1, source_target_pairs={{0,1},{1,0},{2,3},{3,2},{4,5},{5,4},{6,7},{7,6},{8,9},{9,8},{10,11... | collective-permute-start | bytes 491528 | tf_op jit(solution)/shard_map/ppermute | solution.py:50
  127.1 3.8 %collective-permute-start.22 = (f32[80,128]{1,0:T(8,128)S(1)}, f32[80,128]{1,0:T(8,128)S(1)}, u32[]{:S(2)}, u32[]{:S(2)}) collective-permute-start(f32[80,128]{1,0:T(8,128)S(1)} %get-tuple-element.64), channel_id=1, source_target_pairs={{0,6},{1,7},{2,4},{3,5},{4,2},{5,3},{6,0},{7,1},{8,14},{9,15},{10,... | collective-permute-start | bytes 122888 | tf_op jit(solution)/shard_map/ppermute | solution.py:50
  132.1 7.7 %collective-permute-start.25 = (f32[80,128]{1,0:T(8,128)S(1)}, f32[80,128]{1,0:T(8,128)S(1)}, u32[]{:S(2)}, u32[]{:S(2)}) collective-permute-start(f32[80,128]{1,0:T(8,128)S(1)} %fusion.2), channel_id=1, source_target_pairs={{0,24},{8,16},{16,8},{24,0},{1,25},{9,17},{17,9},{25,1},{2,26},{10... | collective-permute-start | bytes 122888 | tf_op jit(solution)/shard_map/ppermute | solution.py:50
  135.5 4.3 %collective-permute-start.26 = (f32[80,128]{1,0:T(8,128)S(1)}, f32[80,128]{1,0:T(8,128)S(1)}, u32[]{:S(2)}, u32[]{:S(2)}) collective-permute-start(f32[80,128]{1,0:T(8,128)S(1)} %fusion.2), channel_id=1, source_target_pairs={{0,16},{8,24},{16,0},{24,8},{1,17},{9,25},{17,1},{25,9},{2,18},{10... | collective-permute-start | bytes 122888 | tf_op jit(solution)/shard_map/ppermute | solution.py:50
  135.5 4.3 %collective-permute-start.27 = (f32[80,128]{1,0:T(8,128)S(1)}, f32[80,128]{1,0:T(8,128)S(1)}, u32[]{:S(2)}, u32[]{:S(2)}) collective-permute-start(f32[80,128]{1,0:T(8,128)S(1)} %fusion.2), channel_id=1, source_target_pairs={{0,8},{8,0},{16,24},{24,16},{1,9},{9,1},{17,25},{25,17},{2,10},{10... | collective-permute-start | bytes 122888 | tf_op jit(solution)/shard_map/ppermute | solution.py:50
  139.8 6.4 %collective-permute-start.29 = (f32[80,128]{1,0:T(8,128)S(1)}, f32[80,128]{1,0:T(8,128)S(1)}, u32[]{:S(2)}, u32[]{:S(2)}) collective-permute-start(f32[80,128]{1,0:T(8,128)S(1)} %add_add_fusion.refs_0_), channel_id=1, source_target_pairs={{0,2},{1,3},{2,0},{3,1},{4,6},{5,7},{6,4},{7,5},{8,10},{9,11},{10,... | collective-permute-start | bytes 122888 | tf_op jit(solution)/shard_map/ppermute | solution.py:50
  140.6 6.1 %collective-permute-start.31 = (f32[80,128]{1,0:T(8,128)S(1)}, f32[80,128]{1,0:T(8,128)S(1)}, u32[]{:S(2)}, u32[]{:S(2)}) collective-permute-start(f32[80,128]{1,0:T(8,128)S(1)} %add_add_fusion.refs_0_), channel_id=1, source_target_pairs={{0,4},{1,5},{2,6},{3,7},{4,0},{5,1},{6,2},{7,3},{8,12},{9,13},{10,... | collective-permute-start | bytes 122888 | tf_op jit(solution)/shard_map/ppermute | solution.py:50
  141.9 5.9 %collective-permute-start.33 = (f32[80,128]{1,0:T(8,128)S(1)}, f32[80,128]{1,0:T(8,128)S(1)}, u32[]{:S(2)}, u32[]{:S(2)}) collective-permute-start(f32[80,128]{1,0:T(8,128)S(1)} %add_add_fusion.refs_0_), channel_id=1, source_target_pairs={{0,6},{1,7},{2,4},{3,5},{4,2},{5,3},{6,0},{7,1},{8,14},{9,15},{10,... | collective-permute-start | bytes 122888 | tf_op jit(solution)/shard_map/ppermute | solution.py:50
  142.5 8.0 %collective-permute-start.28 = (f32[80,128]{1,0:T(8,128)S(1)}, f32[80,128]{1,0:T(8,128)S(1)}, u32[]{:S(2)}, u32[]{:S(2)}) collective-permute-start(f32[80,128]{1,0:T(8,128)S(1)} %add_add_fusion.refs_0_), channel_id=1, source_target_pairs={{0,1},{1,0},{2,3},{3,2},{4,5},{5,4},{6,7},{7,6},{8,9},{9,8},{10,11... | collective-permute-start | bytes 122888 | tf_op jit(solution)/shard_map/ppermute | solution.py:50
  146.2 4.4 %collective-permute-start.30 = (f32[80,128]{1,0:T(8,128)S(1)}, f32[80,128]{1,0:T(8,128)S(1)}, u32[]{:S(2)}, u32[]{:S(2)}) collective-permute-start(f32[80,128]{1,0:T(8,128)S(1)} %collective-permute-done.29.refs_2_), channel_id=1, source_target_pairs={{0,1},{1,0},{2,3},{3,2},{4,5},{5,4},{6,7},{7,6},{8,9},{9,8},{10,11... | collective-permute-start | bytes 122888 | tf_op jit(solution)/shard_map/ppermute | solution.py:50
  146.7 3.9 %collective-permute-start.32 = (f32[80,128]{1,0:T(8,128)S(1)}, f32[80,128]{1,0:T(8,128)S(1)}, u32[]{:S(2)}, u32[]{:S(2)}) collective-permute-start(f32[80,128]{1,0:T(8,128)S(1)} %collective-permute-done.31.refs_4_), channel_id=1, source_target_pairs={{0,1},{1,0},{2,3},{3,2},{4,5},{5,4},{6,7},{7,6},{8,9},{9,8},{10,11... | collective-permute-start | bytes 122888 | tf_op jit(solution)/shard_map/ppermute | solution.py:50
  (44 other events, 281.6 us)
